TPU v7x, 256 devices: a whole 4x4x8 slice. The times are simulated.
256 devices in a mesh: scan: 64 (over x, z, core), tile: 4 (over y).
Axes of the slice: x: 4, y: 4, z: 8, core: 2. Of those that a mesh axis runs over, the one named last changes fastest.
Arguments:
- object_field: float32 [2, 2048, 1024], P(None, 'scan', 'tile'), may hold values from -4.2 to 4.2
- probe: float32 [2, 3, 256, 256], replicated, may hold values from -1.8 to 1.8
- amplitude: float32 [512, 256, 256], P(('scan', 'tile')), may hold values from 0.3 to 3
- positions: int32 [512, 2], replicated, may hold values from -128 to 1919, as said below
- scan_list: int32 [512], P(('scan', 'tile')), may hold values from 0 to 511, as said below
Outputs:
- updated_object: float32 [2, 2048, 1024], P(None, 'scan', 'tile')
- updated_probe: float32 [2, 3, 256, 256], replicated
Inputs may be any that keep to these rules, and one draw needn't show every extreme that they name: positions[k, 0] is a row offset and positions[k, 1] a column offset; column offsets lie in 0 to 768. The position in a slot held by the device with scan index s has a row offset r with s * 32 - 256/2 <= r < (s + 1) * 32 - 256/2. `scan_list`: each position appears in exactly one slot.
All inputs are finite; a program needn't handle non-finite values.
Results may differ from a plain program's by a relative error of at most 0.0001.
Values sent between devices are 32-bit elements; how exact they have to be, the bound alone decides.
A program may use at most 64 MiB of HBM per device.

v0:
```python
import math

import jax
import jax.numpy as jnp
from jax import lax
from jax.sharding import PartitionSpec as P

ITERATIONS = 2


INTENSITY_FLOOR = 0.1
OBJECT_RATE = 0.05
PROBE_RATE = 0.5


def shifted(block, axis, distance):
    devices = range(lax.axis_size(axis))
    route = [(i - distance, i) for i in devices if i - distance in devices]
    return lax.ppermute(block, axis, route)


def dft_tables(length):
    index = jnp.arange(length, dtype=jnp.int32)
    phase = index[:, None] * index[None, :] % length
    angle = phase.astype(jnp.float32) * (-2.0 * math.pi / length)
    scale = 1.0 / math.sqrt(length)
    return (jnp.cos(angle) * scale, jnp.sin(angle) * scale)


def apply_left(table, values):
    return jnp.einsum("kx,mxy->mky", table, values, precision=lax.Precision.HIGHEST)


def apply_right(table, values):
    return jnp.einsum("mky,ly->mkl", values, table, precision=lax.Precision.HIGHEST)


def transform(cosine_table, sine_table, real_part, imag_part):
    left_real = apply_left(cosine_table, real_part) - apply_left(sine_table, imag_part)
    left_imag = apply_left(cosine_table, imag_part) + apply_left(sine_table, real_part)
    out_real = apply_right(cosine_table, left_real) - apply_right(sine_table, left_imag)
    out_imag = apply_right(cosine_table, left_imag) + apply_right(sine_table, left_real)
    return (out_real, out_imag)


def assemble(strip, reach):
    pieces = []
    for offset in range(-reach, reach + 1):
        if offset == 0:
            pieces.append(strip)
        else:
            pieces.append(shifted(strip, "scan", -offset))
    return jnp.concatenate(pieces, axis=1)


def disperse(grads, reach, tile_rows):
    owned = grads[:, reach * tile_rows : (reach + 1) * tile_rows]
    for offset in range(-reach, reach + 1):
        if offset != 0:
            block = grads[:, (offset + reach) * tile_rows : (offset + reach + 1) * tile_rows]
            owned = owned + shifted(block, "scan", offset)
    return owned


def on_device(object_field, probe, amplitude, positions, scan_list):
    tile_rows = object_field.shape[1]
    patch = probe.shape[2]
    reach = patch // (2 * tile_rows)
    total = positions.shape[0]
    cosine_table, sine_table = dft_tables(patch)
    match = scan_list[:, None] == jnp.arange(total, dtype=jnp.int32)[None, :]
    row_offset = jnp.sum(jnp.where(match, positions[None, :, 0], 0), axis=1)
    column_start = jnp.sum(jnp.where(match, positions[None, :, 1], 0), axis=1)
    row_start = row_offset - lax.axis_index("scan") * tile_rows + patch // 2
    field = object_field
    modes = probe
    for rounds in range(ITERATIONS):
        band = assemble(lax.all_gather(field, "tile", axis=2, tiled=True), reach)
        probe_real = modes[0]
        probe_imag = modes[1]

        def visit(carry, item):
            grad_band, grad_modes = carry
            pattern, row_at, column_at = item
            window = lax.dynamic_slice(band, (0, row_at, column_at), (2, patch, patch))
            wave_real = probe_real * window[0] - probe_imag * window[1]
            wave_imag = probe_real * window[1] + probe_imag * window[0]
            far_real, far_imag = transform(cosine_table, sine_table, wave_real, wave_imag)
            power = jnp.sum(far_real * far_real + far_imag * far_imag, axis=0)
            factor = 1.0 - pattern / jnp.sqrt(jnp.maximum(power, INTENSITY_FLOOR))
            back_real, back_imag = transform(
                cosine_table, -sine_table, far_real * factor, far_imag * factor
            )
            term_real = jnp.sum(probe_real * back_real + probe_imag * back_imag, axis=0)
            term_imag = jnp.sum(probe_real * back_imag - probe_imag * back_real, axis=0)
            previous = lax.dynamic_slice(grad_band, (0, row_at, column_at), (2, patch, patch))
            grad_band = lax.dynamic_update_slice(
                grad_band, previous + jnp.stack([term_real, term_imag]), (0, row_at, column_at)
            )
            probe_term = jnp.stack(
                [
                    window[0] * back_real + window[1] * back_imag,
                    window[0] * back_imag - window[1] * back_real,
                ]
            )
            return ((grad_band, grad_modes + probe_term), None)

        start = (jnp.zeros_like(band), jnp.zeros_like(modes))
        (grad_band, grad_modes), unused = lax.scan(
            visit, start, (amplitude, row_start, column_start)
        )
        grad_modes = lax.psum(grad_modes, ("scan", "tile"))
        owned = lax.psum_scatter(
            disperse(grad_band, reach, tile_rows), "tile", scatter_dimension=2, tiled=True
        )
        field = field - OBJECT_RATE * owned
        modes = modes - PROBE_RATE / total * grad_modes
    return (field, modes)


def solution(mesh):
    in_specs = (
        P(None, "scan", "tile"),
        P(),
        P(("scan", "tile"), None, None),
        P(),
        P(("scan", "tile")),
    )
    out_specs = (P(None, "scan", "tile"), P())
    return jax.shard_map(
        on_device, mesh=mesh, in_specs=in_specs, out_specs=out_specs, check_vma=False
    )
```

profile of v0, /device:TPU:1, one launch (start us, length us, event | category | flops | bytes accessed | tf_op | source)
XLA Modules:
  0.0 940.4 jit_solution(10286319883534121954)
XLA Ops:
  8.1 11.5 %all_gather.6 = f32[2,32,1024]{2,1,0:T(8,128)S(1)} all-gather(f32[2,32,256]{2,1,0:T(8,128)} %param.9), channel_id=1, replica_groups=mesh['scan'=64,'tile'=4] {'tile'}, dimensions={2}, use_global_device_ids=true | all-gather | bytes 327680 | tf_op jit(solution)/shard_map/all_gather | solution.py:78
  19.5 4.9 collective-permute-start
  24.4 9.3 collective-permute-start.1
  33.7 2.6 collective-permute-start.2
  56.1 12.7 %collective-permute-done.6 = f32[2,32,1024]{2,1,0:T(8,128)S(1)} collective-permute-done((f32[2,32,1024]{2,1,0:T(8,128)S(1)}, f32[2,32,1024]{2,1,0:T(8,128)S(1)}, u32[]{:S(2)}, u32[]{:S(2)}) %collective-permute-start.6) | collective-permute-done | bytes 262176 | tf_op jit(solution)/shard_map/ppermute | solution.py:19
  69.5 3.0 collective-permute-done.7
  74.9 113.5 %while.30 = (s32[]{:T(128)}, f32[2,288,1024]{2,1,0:T(8,128)}, f32[2,3,256,256]{3,2,1,0:T(8,128)}, s32[2]{0:T(128)S(1)}, s32[2]{0:T(128)S(1)}, /*index=5*/f32[2,2...) while((s32[]{:T(128)}, f32[2,288,1024]{2,1,0:T(8,128)}, ...), condition=%wide.region_6.7_spmd.clone.clone, body=%wide.region_2.6_spmd.clone.clone.sunk | while | flops 9689366528 | bytes 53215532 | solution.py:109
  93.2 2.8 convolution_subtract_fusion.10
  106.0 2.4 fusion.405
  117.4 3.3 add_bitcast_fusion.4
  123.5 6.0 dynamic_update_slice.14
  160.2 2.7 fusion.405
  171.9 3.3 add_bitcast_fusion.4
  175.2 2.8 maximum_add_fusion.9
  179.4 6.2 dynamic_update_slice.14
  191.5 3.0 collective-permute-start.11
  194.5 4.2 collective-permute-start.12
  198.7 2.5 collective-permute-start.13
  201.1 3.7 collective-permute-start.14
  204.9 5.4 collective-permute-start.15
  213.1 6.9 collective-permute-done.15
  220.0 7.1 collective-permute-done.8
  227.1 7.4 collective-permute-done.9
  237.0 22.5 %reduce-scatter.3.cloned.1.call-done = f32[2,32,256]{2,1,0:T(8,128)} async-done(((f32[2,32,1024]{2,1,0:T(8,128)}), f32[2,32,256]{2,1,0:T(8,128)}) %reduce-scatter.3.cloned.1.call-update) | async-done | bytes 65552 | tf_op jit(solution)/shard_map/reduce_scatter | solution.py:113
  260.4 10.8 %all_gather.7 = f32[2,32,1024]{2,1,0:T(8,128)S(1)} all-gather(f32[2,32,256]{2,1,0:T(8,128)S(1)} %multiply_subtract_fusion.9), channel_id=1, replica_groups=mesh['scan'=64,'tile'=4] {'tile'}, dimensions={2}, use_global_device_ids=true | all-gather | bytes 327680 | tf_op jit(solution)/shard_map/all_gather | solution.py:78
  271.2 4.0 collective-permute-start.16
  275.2 10.1 %collective-permute-start.17 = (f32[2,32,1024]{2,1,0:T(8,128)S(1)}, f32[2,32,1024]{2,1,0:T(8,128)S(1)}, u32[]{:S(2)}, u32[]{:S(2)}) collective-permute-start(f32[2,32,1024]{2,1,0:T(8,128)S(1)} %all_gather.7), channel_id=1, source_target_pairs={{0,12},{4,16},{8,20},{12,24},{16,28},{20,32},{24,36},{28,40},{32,4... | collective-permute-start | bytes 786440 | tf_op jit(solution)/shard_map/ppermute | solution.py:19
  292.0 214.6 %all-reduce.3.cloned.1.call-done = f32[2,3,256,256]{3,2,1,0:T(8,128)} async-done(((f32[2,3,256,256]{3,2,1,0:T(8,128)}), f32[2,3,256,256]{3,2,1,0:T(8,128)}) %all-reduce.3.cloned.1.call-update) | async-done | bytes 1572880 | tf_op jit(solution)/shard_map/psum | solution.py:112
  517.3 11.3 %collective-permute-done.22 = f32[2,32,1024]{2,1,0:T(8,128)S(1)} collective-permute-done((f32[2,32,1024]{2,1,0:T(8,128)S(1)}, f32[2,32,1024]{2,1,0:T(8,128)S(1)}, u32[]{:S(2)}, u32[]{:S(2)}) %collective-permute-start.22) | collective-permute-done | bytes 262176 | tf_op jit(solution)/shard_map/ppermute | solution.py:19
  529.3 9.8 %collective-permute-done.23 = f32[2,32,1024]{2,1,0:T(8,128)S(1)} collective-permute-done((f32[2,32,1024]{2,1,0:T(8,128)S(1)}, f32[2,32,1024]{2,1,0:T(8,128)S(1)}, u32[]{:S(2)}, u32[]{:S(2)}) %collective-permute-start.23) | collective-permute-done | bytes 262176 | tf_op jit(solution)/shard_map/ppermute | solution.py:19
  541.6 112.6 %while.31 = (s32[]{:T(128)}, f32[2,288,1024]{2,1,0:T(8,128)}, f32[2,3,256,256]{3,2,1,0:T(8,128)}, s32[2]{0:T(128)S(1)}, s32[2]{0:T(128)S(1)}, /*index=5*/f32[2,2...) while((s32[]{:T(128)}, f32[2,288,1024]{2,1,0:T(8,128)}, ...), condition=%wide.region_13.14_spmd.clone.clone, body=%wide.region_9.13_spmd.clone.clone.sunk | while | flops 9689366528 | bytes 53215532 | solution.py:109
  572.4 2.7 fusion.445
  584.0 3.3 add_bitcast_fusion.5
  590.1 6.0 dynamic_update_slice.15
  614.3 2.6 convolution_subtract_fusion.11
  626.9 2.4 fusion.445
  638.3 3.3 add_bitcast_fusion.5
  641.7 2.9 maximum_add_fusion.11
  645.9 6.2 dynamic_update_slice.15
  654.2 2.6 fusion.268
  662.8 3.9 collective-permute-start.28
  666.7 3.1 collective-permute-done.24
  671.1 4.7 collective-permute-done.25
  675.8 10.5 %collective-permute-start.30 = (f32[2,32,1024]{2,1,0:T(8,128)S(1)}, f32[2,32,1024]{2,1,0:T(8,128)S(1)}, u32[]{:S(2)}, u32[]{:S(2)}) collective-permute-start(f32[2,32,1024]{2,1,0:T(8,128)S(1)} %get-tuple-element.522), channel_id=1, source_target_pairs={{0,12},{4,16},{8,20},{12,24},{16,28},{20,32},{24,36},{28,40},{32,4... | collective-permute-start | bytes 786440 | tf_op jit(solution)/shard_map/ppermute | solution.py:19
  687.8 6.0 collective-permute-done.30
  693.8 7.2 collective-permute-done.31
  702.9 225.7 %all-reduce.5.cloned.1.call-done = f32[2,3,256,256]{3,2,1,0:T(8,128)} async-done(((f32[2,3,256,256]{3,2,1,0:T(8,128)}), f32[2,3,256,256]{3,2,1,0:T(8,128)}) %all-reduce.5.cloned.1.call-update) | async-done | bytes 1572880 | tf_op jit(solution)/shard_map/psum | solution.py:112
  928.6 2.8 multiply_subtract_fusion.6
  (177 shorter events, 209.9 us)
Async XLA Ops:
  8.0 35.0 %copy-start.6 = (s32[2]{0:T(128)S(1)}, s32[2]{0:T(128)}, u32[]{:S(2)}) copy-start(s32[2]{0:T(128)} %param.13) | copy-start | bytes 28
  8.0 251.5 %reduce-scatter.3.cloned.1.call-start = ((), (), s32[]{:S(2)}) async-start(), calls=%async_computation.2 | async-start | bytes 327680 | tf_op jit(solution)/shard_map/reduce_scatter | solution.py:113
  19.5 23.7 %collective-permute-start = (f32[2,32,1024]{2,1,0:T(8,128)S(1)}, f32[2,32,1024]{2,1,0:T(8,128)S(1)}, u32[]{:S(2)}, u32[]{:S(2)}) collective-permute-start(f32[2,32,1024]{2,1,0:T(8,128)S(1)} %all_gather.6), channel_id=1, source_target_pairs={{0,16},{4,20},{8,24},{12,28},{16,32},{20,36},{24,40},{28,44},{32,4... | collective-permute-start | bytes 786440 | tf_op jit(solution)/shard_map/ppermute | solution.py:19
  24.4 21.9 %collective-permute-start.1 = (f32[2,32,1024]{2,1,0:T(8,128)S(1)}, f32[2,32,1024]{2,1,0:T(8,128)S(1)}, u32[]{:S(2)}, u32[]{:S(2)}) collective-permute-start(f32[2,32,1024]{2,1,0:T(8,128)S(1)} %all_gather.6), channel_id=1, source_target_pairs={{0,12},{4,16},{8,20},{12,24},{16,28},{20,32},{24,36},{28,40},{32,4... | collective-permute-start | bytes 786440 | tf_op jit(solution)/shard_map/ppermute | solution.py:19
  33.7 16.6 %collective-permute-start.2 = (f32[2,32,1024]{2,1,0:T(8,128)S(1)}, f32[2,32,1024]{2,1,0:T(8,128)S(1)}, u32[]{:S(2)}, u32[]{:S(2)}) collective-permute-start(f32[2,32,1024]{2,1,0:T(8,128)S(1)} %all_gather.6), channel_id=1, source_target_pairs={{0,8},{4,12},{8,16},{12,20},{16,24},{20,28},{24,32},{28,36},{32,40... | collective-permute-start | bytes 786440 | tf_op jit(solution)/shard_map/ppermute | solution.py:19
  36.4 16.8 %collective-permute-start.3 = (f32[2,32,1024]{2,1,0:T(8,128)S(1)}, f32[2,32,1024]{2,1,0:T(8,128)S(1)}, u32[]{:S(2)}, u32[]{:S(2)}) collective-permute-start(f32[2,32,1024]{2,1,0:T(8,128)S(1)} %all_gather.6), channel_id=1, source_target_pairs={{0,4},{4,8},{8,12},{12,16},{16,20},{20,24},{24,28},{28,32},{32,36}... | collective-permute-start | bytes 786440 | tf_op jit(solution)/shard_map/ppermute | solution.py:19
  38.3 16.3 %collective-permute-start.4 = (f32[2,32,1024]{2,1,0:T(8,128)S(1)}, f32[2,32,1024]{2,1,0:T(8,128)S(1)}, u32[]{:S(2)}, u32[]{:S(2)}) collective-permute-start(f32[2,32,1024]{2,1,0:T(8,128)S(1)} %all_gather.6), channel_id=1, source_target_pairs={{4,0},{8,4},{12,8},{16,12},{20,16},{24,20},{28,24},{32,28},{36,32}... | collective-permute-start | bytes 786440 | tf_op jit(solution)/shard_map/ppermute | solution.py:19
  43.2 12.1 %collective-permute-start.5 = (f32[2,32,1024]{2,1,0:T(8,128)S(1)}, f32[2,32,1024]{2,1,0:T(8,128)S(1)}, u32[]{:S(2)}, u32[]{:S(2)}) collective-permute-start(f32[2,32,1024]{2,1,0:T(8,128)S(1)} %all_gather.6), channel_id=1, source_target_pairs={{8,0},{12,4},{16,8},{20,12},{24,16},{28,20},{32,24},{36,28},{40,32... | collective-permute-start | bytes 786440 | tf_op jit(solution)/shard_map/ppermute | solution.py:19
  46.3 22.4 %collective-permute-start.6 = (f32[2,32,1024]{2,1,0:T(8,128)S(1)}, f32[2,32,1024]{2,1,0:T(8,128)S(1)}, u32[]{:S(2)}, u32[]{:S(2)}) collective-permute-start(f32[2,32,1024]{2,1,0:T(8,128)S(1)} %all_gather.6), channel_id=1, source_target_pairs={{12,0},{16,4},{20,8},{24,12},{28,16},{32,20},{36,24},{40,28},{44,3... | collective-permute-start | bytes 786440 | tf_op jit(solution)/shard_map/ppermute | solution.py:19
  50.4 22.1 %collective-permute-start.7 = (f32[2,32,1024]{2,1,0:T(8,128)S(1)}, f32[2,32,1024]{2,1,0:T(8,128)S(1)}, u32[]{:S(2)}, u32[]{:S(2)}) collective-permute-start(f32[2,32,1024]{2,1,0:T(8,128)S(1)} %all_gather.6), channel_id=1, source_target_pairs={{16,0},{20,4},{24,8},{28,12},{32,16},{36,20},{40,24},{44,28},{48,3... | collective-permute-start | bytes 786440 | tf_op jit(solution)/shard_map/ppermute | solution.py:19
  120.7 1.4 copy-start
  175.2 2.8 copy-start
  190.1 69.4 %copy-start.5 = (f32[2,32,256]{2,1,0:T(8,128)S(1)}, f32[2,32,256]{2,1,0:T(8,128)}, u32[]{:S(2)}) copy-start(f32[2,32,256]{2,1,0:T(8,128)} %param.9) | copy-start | bytes 196612
  190.1 14.8 %collective-permute-start.10 = (f32[2,32,1024]{2,1,0:T(8,128)S(1)}, f32[2,32,1024]{2,1,0:T(8,128)S(1)}, u32[]{:S(2)}, u32[]{:S(2)}) collective-permute-start(f32[2,32,1024]{2,1,0:T(8,128)S(1)} %get-tuple-element.527), channel_id=1, source_target_pairs={{8,0},{12,4},{16,8},{20,12},{24,16},{28,20},{32,24},{36,28},{40,32... | collective-permute-start | bytes 786440 | tf_op jit(solution)/shard_map/ppermute | solution.py:19
  191.5 18.8 %collective-permute-start.11 = (f32[2,32,1024]{2,1,0:T(8,128)S(1)}, f32[2,32,1024]{2,1,0:T(8,128)S(1)}, u32[]{:S(2)}, u32[]{:S(2)}) collective-permute-start(f32[2,32,1024]{2,1,0:T(8,128)S(1)} %get-tuple-element.526), channel_id=1, source_target_pairs={{4,0},{8,4},{12,8},{16,12},{20,16},{24,20},{28,24},{32,28},{36,32}... | collective-permute-start | bytes 786440 | tf_op jit(solution)/shard_map/ppermute | solution.py:19
  194.5 17.1 %collective-permute-start.12 = (f32[2,32,1024]{2,1,0:T(8,128)S(1)}, f32[2,32,1024]{2,1,0:T(8,128)S(1)}, u32[]{:S(2)}, u32[]{:S(2)}) collective-permute-start(f32[2,32,1024]{2,1,0:T(8,128)S(1)} %get-tuple-element.525), channel_id=1, source_target_pairs={{0,4},{4,8},{8,12},{12,16},{16,20},{20,24},{24,28},{28,32},{32,36}... | collective-permute-start | bytes 786440 | tf_op jit(solution)/shard_map/ppermute | solution.py:19
  198.7 14.4 %collective-permute-start.13 = (f32[2,32,1024]{2,1,0:T(8,128)S(1)}, f32[2,32,1024]{2,1,0:T(8,128)S(1)}, u32[]{:S(2)}, u32[]{:S(2)}) collective-permute-start(f32[2,32,1024]{2,1,0:T(8,128)S(1)} %get-tuple-element.531), channel_id=1, source_target_pairs={{0,8},{4,12},{8,16},{12,20},{16,24},{20,28},{24,32},{28,36},{32,40... | collective-permute-start | bytes 786440 | tf_op jit(solution)/shard_map/ppermute | solution.py:19
  201.1 11.9 %collective-permute-start.14 = (f32[2,32,1024]{2,1,0:T(8,128)S(1)}, f32[2,32,1024]{2,1,0:T(8,128)S(1)}, u32[]{:S(2)}, u32[]{:S(2)}) collective-permute-start(f32[2,32,1024]{2,1,0:T(8,128)S(1)} %get-tuple-element.530), channel_id=1, source_target_pairs={{0,12},{4,16},{8,20},{12,24},{16,28},{20,32},{24,36},{28,40},{32,4... | collective-permute-start | bytes 786440 | tf_op jit(solution)/shard_map/ppermute | solution.py:19
  204.9 15.1 %collective-permute-start.15 = (f32[2,32,1024]{2,1,0:T(8,128)S(1)}, f32[2,32,1024]{2,1,0:T(8,128)S(1)}, u32[]{:S(2)}, u32[]{:S(2)}) collective-permute-start(f32[2,32,1024]{2,1,0:T(8,128)S(1)} %get-tuple-element.529), channel_id=1, source_target_pairs={{0,16},{4,20},{8,24},{12,28},{16,32},{20,36},{24,40},{28,44},{32,4... | collective-permute-start | bytes 786440 | tf_op jit(solution)/shard_map/ppermute | solution.py:19
  210.3 16.8 %collective-permute-start.8 = (f32[2,32,1024]{2,1,0:T(8,128)S(1)}, f32[2,32,1024]{2,1,0:T(8,128)S(1)}, u32[]{:S(2)}, u32[]{:S(2)}) collective-permute-start(f32[2,32,1024]{2,1,0:T(8,128)S(1)} %get-tuple-element.524), channel_id=1, source_target_pairs={{16,0},{20,4},{24,8},{28,12},{32,16},{36,20},{40,24},{44,28},{48,3... | collective-permute-start | bytes 786440 | tf_op jit(solution)/shard_map/ppermute | solution.py:19
  211.6 295.0 %copy-start.4 = (f32[2,3,256,256]{3,2,1,0:T(8,128)S(1)}, f32[2,3,256,256]{3,2,1,0:T(8,128)}, u32[]{:S(2)}) copy-start(f32[2,3,256,256]{3,2,1,0:T(8,128)} %param.10) | copy-start | bytes 4718596
  211.6 22.9 %collective-permute-start.9 = (f32[2,32,1024]{2,1,0:T(8,128)S(1)}, f32[2,32,1024]{2,1,0:T(8,128)S(1)}, u32[]{:S(2)}, u32[]{:S(2)}) collective-permute-start(f32[2,32,1024]{2,1,0:T(8,128)S(1)} %get-tuple-element.528), channel_id=1, source_target_pairs={{12,0},{16,4},{20,8},{24,12},{28,16},{32,20},{36,24},{40,28},{44,3... | collective-permute-start | bytes 786440 | tf_op jit(solution)/shard_map/ppermute | solution.py:19
  236.3 270.2 %all-reduce.3.cloned.1.call-start = ((), (), s32[]{:S(2)}) async-start(), calls=%async_computation.3 | async-start | bytes 3145728 | tf_op jit(solution)/shard_map/psum | solution.py:112
  236.9 691.7 %all-reduce.5.cloned.1.call-start = ((), (), s32[]{:S(2)}) async-start(), calls=%async_computation.5 | async-start | bytes 3145728 | tf_op jit(solution)/shard_map/psum | solution.py:112
  271.2 237.1 %collective-permute-start.16 = (f32[2,32,1024]{2,1,0:T(8,128)S(1)}, f32[2,32,1024]{2,1,0:T(8,128)S(1)}, u32[]{:S(2)}, u32[]{:S(2)}) collective-permute-start(f32[2,32,1024]{2,1,0:T(8,128)S(1)} %all_gather.7), channel_id=1, source_target_pairs={{0,16},{4,20},{8,24},{12,28},{16,32},{20,36},{24,40},{28,44},{32,4... | collective-permute-start | bytes 786440 | tf_op jit(solution)/shard_map/ppermute | solution.py:19
  275.2 235.2 %collective-permute-start.17 = (f32[2,32,1024]{2,1,0:T(8,128)S(1)}, f32[2,32,1024]{2,1,0:T(8,128)S(1)}, u32[]{:S(2)}, u32[]{:S(2)}) collective-permute-start(f32[2,32,1024]{2,1,0:T(8,128)S(1)} %all_gather.7), channel_id=1, source_target_pairs={{0,12},{4,16},{8,20},{12,24},{16,28},{20,32},{24,36},{28,40},{32,4... | collective-permute-start | bytes 786440 | tf_op jit(solution)/shard_map/ppermute | solution.py:19
  285.3 227.1 %collective-permute-start.18 = (f32[2,32,1024]{2,1,0:T(8,128)S(1)}, f32[2,32,1024]{2,1,0:T(8,128)S(1)}, u32[]{:S(2)}, u32[]{:S(2)}) collective-permute-start(f32[2,32,1024]{2,1,0:T(8,128)S(1)} %all_gather.7), channel_id=1, source_target_pairs={{0,8},{4,12},{8,16},{12,20},{16,24},{20,28},{24,32},{28,36},{32,40... | collective-permute-start | bytes 786440 | tf_op jit(solution)/shard_map/ppermute | solution.py:19
  287.6 226.8 %collective-permute-start.19 = (f32[2,32,1024]{2,1,0:T(8,128)S(1)}, f32[2,32,1024]{2,1,0:T(8,128)S(1)}, u32[]{:S(2)}, u32[]{:S(2)}) collective-permute-start(f32[2,32,1024]{2,1,0:T(8,128)S(1)} %all_gather.7), channel_id=1, source_target_pairs={{0,4},{4,8},{8,12},{12,16},{16,20},{20,24},{24,28},{28,32},{32,36}... | collective-permute-start | bytes 786440 | tf_op jit(solution)/shard_map/ppermute | solution.py:19
  289.7 226.1 %collective-permute-start.20 = (f32[2,32,1024]{2,1,0:T(8,128)S(1)}, f32[2,32,1024]{2,1,0:T(8,128)S(1)}, u32[]{:S(2)}, u32[]{:S(2)}) collective-permute-start(f32[2,32,1024]{2,1,0:T(8,128)S(1)} %all_gather.7), channel_id=1, source_target_pairs={{4,0},{8,4},{12,8},{16,12},{20,16},{24,20},{28,24},{32,28},{36,32}... | collective-permute-start | bytes 786440 | tf_op jit(solution)/shard_map/ppermute | solution.py:19
  508.2 6.2 copy-start.2
  508.3 8.2 collective-permute-start.21
  510.3 18.2 %collective-permute-start.22 = (f32[2,32,1024]{2,1,0:T(8,128)S(1)}, f32[2,32,1024]{2,1,0:T(8,128)S(1)}, u32[]{:S(2)}, u32[]{:S(2)}) collective-permute-start(f32[2,32,1024]{2,1,0:T(8,128)S(1)} %all_gather.7), channel_id=1, source_target_pairs={{12,0},{16,4},{20,8},{24,12},{28,16},{32,20},{36,24},{40,28},{44,3... | collective-permute-start | bytes 786440 | tf_op jit(solution)/shard_map/ppermute | solution.py:19
  512.4 26.8 %collective-permute-start.23 = (f32[2,32,1024]{2,1,0:T(8,128)S(1)}, f32[2,32,1024]{2,1,0:T(8,128)S(1)}, u32[]{:S(2)}, u32[]{:S(2)}) collective-permute-start(f32[2,32,1024]{2,1,0:T(8,128)S(1)} %all_gather.7), channel_id=1, source_target_pairs={{16,0},{20,4},{24,8},{28,12},{32,16},{36,20},{40,24},{44,28},{48,3... | collective-permute-start | bytes 786440 | tf_op jit(solution)/shard_map/ppermute | solution.py:19
  587.4 1.4 copy-start.1
  641.7 2.9 copy-start.1
  656.8 271.8 %copy-start.3 = (f32[2,3,256,256]{3,2,1,0:T(8,128)S(1)}, f32[2,3,256,256]{3,2,1,0:T(8,128)}, u32[]{:S(2)}) copy-start(f32[2,3,256,256]{3,2,1,0:T(8,128)} %copy-done.2) | copy-start | bytes 4718596
  656.8 13.0 %collective-permute-start.24 = (f32[2,32,1024]{2,1,0:T(8,128)}, f32[2,32,1024]{2,1,0:T(8,128)S(1)}, u32[]{:S(2)}, u32[]{:S(2)}) collective-permute-start(f32[2,32,1024]{2,1,0:T(8,128)} %get-tuple-element.516), channel_id=1, source_target_pairs={{16,0},{20,4},{24,8},{28,12},{32,16},{36,20},{40,24},{44,28},{48,3... | collective-permute-start | bytes 786440 | tf_op jit(solution)/shard_map/ppermute | solution.py:19
  658.2 17.6 %collective-permute-start.25 = (f32[2,32,1024]{2,1,0:T(8,128)}, f32[2,32,1024]{2,1,0:T(8,128)S(1)}, u32[]{:S(2)}, u32[]{:S(2)}) collective-permute-start(f32[2,32,1024]{2,1,0:T(8,128)} %get-tuple-element.520), channel_id=1, source_target_pairs={{12,0},{16,4},{20,8},{24,12},{28,16},{32,20},{36,24},{40,28},{44,3... | collective-permute-start | bytes 786440 | tf_op jit(solution)/shard_map/ppermute | solution.py:19
  659.5 26.8 %collective-permute-start.26 = (f32[2,32,1024]{2,1,0:T(8,128)}, f32[2,32,1024]{2,1,0:T(8,128)S(1)}, u32[]{:S(2)}, u32[]{:S(2)}) collective-permute-start(f32[2,32,1024]{2,1,0:T(8,128)} %get-tuple-element.519), channel_id=1, source_target_pairs={{8,0},{12,4},{16,8},{20,12},{24,16},{28,20},{32,24},{36,28},{40,32... | collective-permute-start | bytes 786440 | tf_op jit(solution)/shard_map/ppermute | solution.py:19
  660.8 270.5 %reduce-scatter.5.cloned.1.call-start = ((), (), s32[]{:S(2)}) async-start(), calls=%async_computation.4 | async-start | bytes 327680 | tf_op jit(solution)/shard_map/reduce_scatter | solution.py:113
  660.9 26.9 %collective-permute-start.27 = (f32[2,32,1024]{2,1,0:T(8,128)}, f32[2,32,1024]{2,1,0:T(8,128)S(1)}, u32[]{:S(2)}, u32[]{:S(2)}) collective-permute-start(f32[2,32,1024]{2,1,0:T(8,128)} %get-tuple-element.518), channel_id=1, source_target_pairs={{4,0},{8,4},{12,8},{16,12},{20,16},{24,20},{28,24},{32,28},{36,32}... | collective-permute-start | bytes 786440 | tf_op jit(solution)/shard_map/ppermute | solution.py:19
  662.8 25.0 %collective-permute-start.28 = (f32[2,32,1024]{2,1,0:T(8,128)S(1)}, f32[2,32,1024]{2,1,0:T(8,128)S(1)}, u32[]{:S(2)}, u32[]{:S(2)}) collective-permute-start(f32[2,32,1024]{2,1,0:T(8,128)S(1)} %get-tuple-element.517), channel_id=1, source_target_pairs={{0,4},{4,8},{8,12},{12,16},{16,20},{20,24},{24,28},{28,32},{32,36}... | collective-permute-start | bytes 786440 | tf_op jit(solution)/shard_map/ppermute | solution.py:19
  669.8 18.1 %collective-permute-start.29 = (f32[2,32,1024]{2,1,0:T(8,128)S(1)}, f32[2,32,1024]{2,1,0:T(8,128)S(1)}, u32[]{:S(2)}, u32[]{:S(2)}) collective-permute-start(f32[2,32,1024]{2,1,0:T(8,128)S(1)} %get-tuple-element.523), channel_id=1, source_target_pairs={{0,8},{4,12},{8,16},{12,20},{16,24},{20,28},{24,32},{28,36},{32,40... | collective-permute-start | bytes 786440 | tf_op jit(solution)/shard_map/ppermute | solution.py:19
  675.8 18.0 %collective-permute-start.30 = (f32[2,32,1024]{2,1,0:T(8,128)S(1)}, f32[2,32,1024]{2,1,0:T(8,128)S(1)}, u32[]{:S(2)}, u32[]{:S(2)}) collective-permute-start(f32[2,32,1024]{2,1,0:T(8,128)S(1)} %get-tuple-element.522), channel_id=1, source_target_pairs={{0,12},{4,16},{8,20},{12,24},{16,28},{20,32},{24,36},{28,40},{32,4... | collective-permute-start | bytes 786440 | tf_op jit(solution)/shard_map/ppermute | solution.py:19
  686.3 14.7 %collective-permute-start.31 = (f32[2,32,1024]{2,1,0:T(8,128)S(1)}, f32[2,32,1024]{2,1,0:T(8,128)S(1)}, u32[]{:S(2)}, u32[]{:S(2)}) collective-permute-start(f32[2,32,1024]{2,1,0:T(8,128)S(1)} %get-tuple-element.521), channel_id=1, source_target_pairs={{0,16},{4,20},{8,24},{12,28},{16,32},{20,36},{24,40},{28,44},{32,4... | collective-permute-start | bytes 786440 | tf_op jit(solution)/shard_map/ppermute | solution.py:19
Sparse Core Ops, SparseCore 0:
  236.5 22.9 reduce-scatter.2
  703.0 25.5 reduce-scatter.4
Sparse Core Ops, SparseCore 1:
  243.6 262.9 all-reduce.2
  660.9 267.6 all-reduce.4
where the time goes:
time: 946 us; the launch traced here: 940 us
  waiting for transfers between devices  547 us (58%)
  matrix products  152 us (16%)
  starting transfers between devices  95.8 us (10%)
  local copies, waits for them, and re-layouts  57.8 us (6%)
  other arithmetic  28.4 us (3%)
  blocking collectives  22.3 us (2%)
  loops' own time  21.9 us (2%)
  between operations  16.1 us (2%)
    psum x2, waiting for transfers between devices, on_device(): grad_modes = lax.psum(grad_modes, ('scan', 'tile'))  440 us
    ppermute x32, starting transfers between devices, shifted(): return lax.ppermute(block, axis, route)  95.6 us
    ppermute x32, waiting for transfers between devices, shifted(): return lax.ppermute(block, axis, route)  83.2 us
    dot_general x32, matrix products, apply_right(): jnp.einsum('mky,ly->mkl', values, table, precision=lax.Precision.HIGHEST)  76.7 us
    dot_general x32, matrix products, apply_left(): jnp.einsum('kx,mxy->mky', table, values, precision=lax.Precision.HIGHEST)  75 us
    dynamic_update_slice x4, local copies, waits for them, and re-layouts, visit(): lax.dynamic_update_slice(grad_band, previous + jnp.stack([term_real, term...  24.2 us
    reduce_scatter x2, waiting for transfers between devices, on_device(): lax.psum_scatter(disperse(grad_band, reach, tile_rows), 'tile', scatter_d...  22.5 us
    all_gather x2, blocking collectives, on_device(): band = assemble(lax.all_gather(field, 'tile', axis=2, tiled=True), reach)  22.3 us
  transfers between devices with their start and end apart: 36, of which 17 were waited for; matrix products, arithmetic and copies ran while one was open for 2% of the time, Pallas kernels for 0%

commit v1 on v0

v1 whole, which is shorter than its diff:
```python
import functools
import math

import jax
import jax.numpy as jnp
import ml_dtypes
import numpy as np
from jax import lax
from jax.experimental import pallas as pl
from jax.experimental.pallas import tpu as pltpu
from jax.sharding import PartitionSpec as P

ITERATIONS = 2
INTENSITY_FLOOR = 0.1
OBJECT_RATE = 0.05
PROBE_RATE = 0.5

CORES = 2
CHIPS_Z = 8
LANES = 128
MESH = pl.DeviceIdType.MESH
VMEM_LIMIT = 48 * 1024 * 1024


def dft_tables(length):
    index = np.arange(length)
    angle = (np.outer(index, index) % length) * (-2.0 * math.pi / length)
    scale = 1.0 / math.sqrt(length)
    cosine, sine = np.cos(angle) * scale, np.sin(angle) * scale
    forward = np.block([[cosine, sine], [-sine, cosine]])
    tables = []
    for table in (forward, forward.T):
        high = table.astype(ml_dtypes.bfloat16)
        low = (table - high.astype(np.float64)).astype(ml_dtypes.bfloat16)
        tables += [high, low]
    return np.stack(tables)


def halves(values):
    high = values.astype(jnp.bfloat16)
    low = (values - high.astype(jnp.float32)).astype(jnp.bfloat16)
    return high, low


def product(left, right):
    dot = functools.partial(jnp.dot, preferred_element_type=jnp.float32)
    return dot(left[0], right[0]) + (dot(left[0], right[1]) + dot(left[1], right[0]))


def sublane(shape):
    return lax.broadcasted_iota(jnp.int32, shape, 1)


def read_rows(values, inside):
    turned = pltpu.roll(values, lax.rem(8 - inside, 8), 1)
    return jnp.where(sublane(turned[1:].shape) < 8 - inside, turned[:-1], turned[1:])


def place_rows(values, inside):
    turned = pltpu.roll(values, inside, 1)
    edge = jnp.zeros((1,) + values.shape[1:], values.dtype)
    before = jnp.concatenate([edge, turned], axis=0)
    after = jnp.concatenate([turned, edge], axis=0)
    return jnp.where(sublane(before.shape) < inside, before, after)


def slots_kernel(
    rows_ref, window_ref, modes_ref, amplitude_ref, table_ref, grad_ref, grad_modes_ref, patch_ref
):
    slots, _, band, patch = window_ref.shape
    count = modes_ref.shape[1]
    forward = (table_ref[0], table_ref[1])
    inverse = (table_ref[2], table_ref[3])
    margin = band - patch
    for slot in range(slots):
        row = rows_ref[slot]
        first = pl.multiple_of((row // 8) * 8, 8)
        inside = row - first
        for part in range(2):
            rows = window_ref[slot, part, pl.ds(first, patch + 8), :].reshape(patch // 8 + 1, 8, patch)
            patch_ref[part] = read_rows(rows, inside).reshape(patch, patch)
            grad_ref[slot, part, :margin, :] = jnp.zeros((margin, patch), jnp.float32)
            grad_ref[slot, part, patch:, :] = jnp.zeros((margin, patch), jnp.float32)
        power = None
        far = []
        for m in range(count):
            patch_real, patch_imag = patch_ref[0], patch_ref[1]
            mode_real, mode_imag = modes_ref[0, m], modes_ref[1, m]
            wave = jnp.concatenate(
                [
                    mode_real * patch_real - mode_imag * patch_imag,
                    mode_real * patch_imag + mode_imag * patch_real,
                ],
                axis=1,
            )
            right = product(halves(wave), forward)
            right = jnp.concatenate([right[:, :patch], right[:, patch:]], axis=0)
            left = product(inverse, halves(right))
            far.append(left)
            square = left * left
            square = square[:patch] + square[patch:]
            power = square if power is None else power + square
        factor = 1.0 - amplitude_ref[slot] * lax.rsqrt(jnp.maximum(power, INTENSITY_FLOOR))
        factor = jnp.concatenate([factor, factor], axis=0)
        term_real = term_imag = None
        for m in range(count):
            left = product(forward, halves(far[m] * factor))
            left = jnp.concatenate([left[:patch], left[patch:]], axis=1)
            back = product(halves(left), inverse)
            back_real, back_imag = back[:, :patch], back[:, patch:]
            patch_real, patch_imag = patch_ref[0], patch_ref[1]
            mode_real, mode_imag = modes_ref[0, m], modes_ref[1, m]
            real = mode_real * back_real + mode_imag * back_imag
            imag = mode_real * back_imag - mode_imag * back_real
            term_real = real if term_real is None else term_real + real
            term_imag = imag if term_imag is None else term_imag + imag
            probe_real = patch_real * back_real + patch_imag * back_imag
            probe_imag = patch_real * back_imag - patch_imag * back_real
            if slot == 0:
                grad_modes_ref[0, m] = probe_real
                grad_modes_ref[1, m] = probe_imag
            else:
                grad_modes_ref[0, m] += probe_real
                grad_modes_ref[1, m] += probe_imag
        for part, term in enumerate((term_real, term_imag)):
            term = place_rows(term.reshape(patch // 8, 8, patch), inside)
            grad_ref[slot, part, pl.ds(first, patch + 8), :] = term.reshape(patch + 8, patch)


def slot_gradients(rows, windows, modes, amplitude, tables):
    slots, _, band, patch = windows.shape
    count = modes.shape[1]
    vmem = pl.BlockSpec(memory_space=pltpu.VMEM)
    return pl.pallas_call(
        slots_kernel,
        out_shape=(
            jax.ShapeDtypeStruct(windows.shape, jnp.float32),
            jax.ShapeDtypeStruct(modes.shape, jnp.float32),
        ),
        in_specs=[pl.BlockSpec(memory_space=pltpu.SMEM), vmem, vmem, vmem, vmem],
        out_specs=(vmem, vmem),
        scratch_shapes=[pltpu.VMEM((2, patch, patch), jnp.float32)],
        compiler_params=pltpu.CompilerParams(vmem_limit_bytes=VMEM_LIMIT),
        cost_estimate=pl.CostEstimate(
            flops=slots * count * 48 * 2 * patch**3,
            bytes_accessed=4 * (2 * windows.size + 2 * modes.size + amplitude.size),
            transcendentals=slots * patch * patch,
        ),
    )(rows, windows, modes, amplitude, tables)


class Place:
    def __init__(self, chips_z):
        self.scan = lax.axis_index("scan")
        self.tile = lax.axis_index("tile")
        self.scans = lax.axis_size("scan")
        self.tiles = lax.axis_size("tile")
        self.chips_z = chips_z
        self.chips_x = self.scans // (chips_z * CORES)
        self.core = lax.rem(self.scan, CORES)
        self.z = lax.rem(self.scan // CORES, chips_z)
        self.x = self.scan // (CORES * chips_z)

    def at_core(self):
        return (self.scan + 1 - 2 * self.core, self.tile)

    def ring_x(self, k):
        x = lax.rem(self.x + k, self.chips_x)
        return x, ((x * self.chips_z + self.z) * CORES + self.core, self.tile)

    def ring_z(self, k):
        z = lax.rem(self.z + k, self.chips_z)
        return z, ((self.x * self.chips_z + z) * CORES + self.core, self.tile)

    def ring_tile(self, k):
        tile = lax.rem(self.tile + k, self.tiles)
        return tile, (self.scan, tile)

    def near(self, d):
        other = self.scan + d
        return jnp.logical_and(other >= 0, other < self.scans), (other, self.tile)


def distances(reach):
    far_first = sorted(range(1, reach + 1), reverse=True)
    return [sign * d for d in far_first for sign in (1, -1)]


def greet(partners):
    barrier = pltpu.get_barrier_semaphore()
    total = 0
    for condition, device in partners:
        if condition is None:
            pl.semaphore_signal(barrier, inc=1, device_id=device, device_id_type=MESH)
            total = total + 1
        else:

            @pl.when(condition)
            def _(device=device):
                pl.semaphore_signal(barrier, inc=1, device_id=device, device_id_type=MESH)

            total = total + condition.astype(jnp.int32)
    pl.semaphore_wait(barrier, total)


def remote(src, dst, sems, at, device):
    return pltpu.make_async_remote_copy(
        src_ref=src,
        dst_ref=dst,
        send_sem=sems[0].at[at],
        recv_sem=sems[1].at[at],
        device_id=device,
        device_id_type=MESH,
    )


def gather_kernel(reach, chips_z, exchange, *refs):
    if exchange:
        (field_ref, columns_ref, window_ref, table_ref, strip, outgoing, columns, tile_send, tile_recv,
         scan_send, scan_recv, column_send, column_recv, local_sem) = refs
    else:
        (field_ref, columns, window_ref, strip, outgoing, tile_send, tile_recv, scan_send, scan_recv) = refs
    place = Place(chips_z)
    _, rows, width = field_ref.shape
    order = distances(reach)
    tile_sems, scan_sems = (tile_send, tile_recv), (scan_send, scan_recv)
    greet(
        [(None, place.ring_tile(k)[1]) for k in range(1, place.tiles)]
        + [place.near(d) for d in order]
    )
    own = pl.ds(pl.multiple_of(place.tile * width, LANES), width)
    gathers = [
        remote(field_ref, strip.at[:, :, own], tile_sems, k - 1, place.ring_tile(k)[1])
        for k in range(1, place.tiles)
    ]
    for copy in gathers:
        copy.start()
    notes = []
    if exchange:
        table_ref[reach] = columns_ref[...]
        for at, d in enumerate(order):
            exists, device = place.near(d)
            note = remote(columns_ref, table_ref.at[reach - d], (column_send, column_recv), at, device)
            pl.when(exists)(note.start)
            notes.append((exists, place.near(-d)[0], note))
    strip[:, :, own] = field_ref[...]
    pad = strip.shape[2] - width * place.tiles
    strip[:, :, width * place.tiles :] = jnp.zeros((2, rows, pad), jnp.float32)
    for at, d in enumerate(order):
        exists, _ = place.near(-d)

        @pl.when(jnp.logical_not(exists))
        def _(d=d):
            window_ref[:, :, (reach - d) * rows : (reach - d + 1) * rows, :] = jnp.zeros(
                (window_ref.shape[0], 2, rows, window_ref.shape[3]), jnp.float32
            )
            if exchange:
                table_ref[reach - d] = jnp.zeros(columns_ref.shape, jnp.int32)

    for exists, from_exists, note in notes:
        pl.when(exists)(note.wait_send)
        pl.when(from_exists)(note.wait_recv)
    if exchange:
        local = pltpu.make_async_copy(table_ref, columns, local_sem)
        local.start()
        local.wait()
    for copy in gathers:
        copy.wait()

    lane = lax.broadcasted_iota(jnp.int32, (rows, LANES), 1)

    def cut(at, target):
        for slot in range(window_ref.shape[0]):
            column = columns[at, 0, slot] if exchange else columns[at, slot]
            first = column // LANES
            inside = column - first * LANES
            for part in range(2):
                pieces = []
                for i in range(width // LANES + 1):
                    piece = strip[part, :, LANES * i : LANES * (i + 1)]
                    for block in range(1, (place.tiles - 1) * width // LANES + 1):
                        at_block = strip[part, :, LANES * (block + i) : LANES * (block + i + 1)]
                        piece = jnp.where(first == block, at_block, piece)
                    pieces.append(pltpu.roll(piece, lax.rem(LANES - inside, LANES), 1))
                for i in range(width // LANES):
                    target[slot, part, :, LANES * i : LANES * (i + 1)] = jnp.where(
                        lane < LANES - inside, pieces[i], pieces[i + 1]
                    )

    sends = []
    for at, d in enumerate(order):
        exists, device = place.near(d)
        copy = remote(
            outgoing.at[at],
            window_ref.at[:, :, (reach - d) * rows : (reach - d + 1) * rows, :],
            scan_sems,
            at,
            device,
        )

        @pl.when(exists)
        def _(at=at, d=d, copy=copy):
            cut(reach + d, outgoing.at[at])
            copy.start()

        sends.append((exists, place.near(-d)[0], copy))
    cut(reach, window_ref.at[:, :, reach * rows : (reach + 1) * rows, :])
    for exists, from_exists, copy in sends:
        pl.when(exists)(copy.wait_send)
        pl.when(from_exists)(copy.wait_recv)


def gather_windows(field, columns, reach, slots, patch, chips_z, exchange, collective_id):
    _, rows, width = field.shape
    tiles = lax.axis_size("tile")
    vmem = pl.BlockSpec(memory_space=pltpu.VMEM)
    smem = pl.BlockSpec(memory_space=pltpu.SMEM)
    near = 2 * reach
    dma = pltpu.SemaphoreType.DMA
    window = jax.ShapeDtypeStruct((slots, 2, (near + 1) * rows, patch), jnp.float32)
    scratch = [
        pltpu.VMEM((2, rows, width * tiles + LANES), jnp.float32),
        pltpu.VMEM((near, slots, 2, rows, patch), jnp.float32),
    ]
    sems = [dma((tiles - 1,)), dma((tiles - 1,)), dma((near,)), dma((near,))]
    if exchange:
        table = (near + 1,) + columns.shape
        out_shape = (window, jax.ShapeDtypeStruct(table, jnp.int32))
        out_specs = (vmem, vmem)
        scratch += [pltpu.SMEM(table, jnp.int32)] + sems + [dma((near,)), dma((near,)), dma(())]
    else:
        out_shape, out_specs = window, vmem
        scratch += sems
    return pl.pallas_call(
        functools.partial(gather_kernel, reach, chips_z, exchange),
        out_shape=out_shape,
        in_specs=[vmem, vmem if exchange else smem],
        out_specs=out_specs,
        scratch_shapes=scratch,
        compiler_params=pltpu.CompilerParams(
            collective_id=collective_id, has_side_effects=True, vmem_limit_bytes=VMEM_LIMIT
        ),
    )(field, columns)


def reduce_kernel(
    reach, chips_z, owners, rate, columns, grad_ref, grad_modes_ref, field_ref, modes_ref,
    new_field_ref, new_modes_ref, arrived, strip, tile_parts, core_part, core_sum, x_parts, x_sum,
    y_parts, y_sum, z_parts, scan_send, scan_recv, tile_send, tile_recv, core_send, core_recv,
    x_send, x_recv, y_send, y_recv, z_send, z_recv, zg_send, zg_recv, yg_send, yg_recv,
    xg_send, xg_recv, cg_send, cg_recv,
):
    place = Place(chips_z)
    _, rows, width = field_ref.shape
    slots = grad_ref.shape[0]
    order = distances(reach)
    xs, ys, zs = place.chips_x, place.tiles, place.chips_z
    half = grad_modes_ref.shape[0] // CORES
    quarter = half // xs
    part = quarter // ys
    piece = part // owners
    owner = place.z < owners

    partners = [(None, place.at_core())]
    partners += [(None, place.ring_x(k)[1]) for k in range(1, xs)]
    partners += [(None, place.ring_tile(k)[1]) for k in range(1, ys)]
    for k in range(1, zs):
        z, device = place.ring_z(k)
        partners.append((jnp.logical_or(owner, z < owners), device))
    partners += [place.near(d) for d in order]
    greet(partners)

    def rows_at(start, size):
        return pl.ds(pl.multiple_of(start, 8), size)

    mine, other = place.core * half, (1 - place.core) * half
    core_copies = []
    for k in list(range(1, xs)) + [0]:
        x = lax.rem(place.x + k, xs)
        copy = remote(
            grad_modes_ref.at[rows_at(other + x * quarter, quarter)],
            core_part.at[rows_at(x * quarter, quarter)],
            (core_send, core_recv), k, place.at_core(),
        )
        copy.start()
        core_copies.append(copy)

    sends = []
    for at, d in enumerate(order):
        exists, device = place.near(d)
        copy = remote(
            grad_ref.at[:, :, (reach + d) * rows : (reach + d + 1) * rows, :],
            arrived.at[reach - d], (scan_send, scan_recv), at, device,
        )
        pl.when(exists)(copy.start)
        from_exists = place.near(-d)[0]

        @pl.when(jnp.logical_not(from_exists))
        def _(d=d):
            arrived[reach - d] = jnp.zeros(arrived.shape[1:], jnp.float32)

        sends.append((exists, from_exists, copy))

    x_copies = []
    for k, copy in zip(list(range(1, xs)) + [0], core_copies):
        copy.wait_recv()
        x, device = place.ring_x(k)
        at = rows_at(x * quarter, quarter)
        core_sum[at, :] = core_part[at, :] + grad_modes_ref[rows_at(mine + x * quarter, quarter), :]
        if k:
            copy = remote(core_sum.at[at], x_parts.at[k - 1], (x_send, x_recv), k - 1, device)
            copy.start()
            x_copies.append(copy)
    arrived[reach] = grad_ref[:, :, reach * rows : (reach + 1) * rows, :]
    for copy in x_copies:
        copy.wait_recv()
    total = core_sum[rows_at(place.x * quarter, quarter), :]
    for k in range(xs - 1):
        total = total + x_parts[k]
    x_sum[...] = total
    y_copies = []
    for k in range(1, ys):
        y, device = place.ring_tile(k)
        copy = remote(x_sum.at[rows_at(y * part, part)], y_parts.at[k - 1], (y_send, y_recv), k - 1, device)
        copy.start()
        y_copies.append(copy)
    for copy in y_copies:
        copy.wait_recv()
    total = x_sum[rows_at(place.tile * part, part), :]
    for k in range(ys - 1):
        total = total + y_parts[k]
    y_sum[...] = total
    z_copies = []
    for k in range(1, zs):
        z, device = place.ring_z(k)
        start = jnp.minimum(z, owners - 1) * piece
        copy = remote(y_sum.at[rows_at(start, piece)], z_parts.at[k - 1], (z_send, z_recv), k - 1, device)
        pl.when(z < owners)(copy.start)
        z_copies.append((z < owners, copy))

    for exists, from_exists, copy in sends:
        pl.when(from_exists)(copy.wait_recv)
    lane = lax.broadcasted_iota(jnp.int32, (rows, LANES), 1)
    blocks = width * ys // LANES
    strip[...] = jnp.zeros(strip.shape, jnp.float32)

    def place_window(index, carry):
        source, slot = index // slots, lax.rem(index, slots)
        column = columns[source, slot]
        first = column // LANES
        inside = column - first * LANES
        for p in range(2):
            values = [
                pltpu.roll(arrived[source, slot, p, :, LANES * i : LANES * (i + 1)], inside, 1)
                for i in range(width // LANES)
            ]
            values = [jnp.zeros_like(values[0])] + values + [jnp.zeros_like(values[0])]
            shifted = [
                jnp.where(lane < inside, values[i], values[i + 1]) for i in range(width // LANES + 1)
            ]
            for block in range(blocks):
                term = jnp.zeros_like(values[0])
                for i, value in enumerate(shifted):
                    term = jnp.where(first + i == block, value, term)
                strip[p, :, LANES * block : LANES * (block + 1)] += term
        return carry

    lax.fori_loop(0, arrived.shape[0] * slots, place_window, 0)
    tile_copies = []
    for k in range(1, ys):
        y, device = place.ring_tile(k)
        copy = remote(
            strip.at[:, :, pl.ds(pl.multiple_of(y * width, LANES), width)],
            tile_parts.at[k - 1], (tile_send, tile_recv), k - 1, device,
        )
        copy.start()
        tile_copies.append(copy)

    my_quarter = mine + place.x * quarter
    my_part = my_quarter + place.tile * part
    my_piece = jnp.minimum(place.z, owners - 1) * piece

    @pl.when(owner)
    def _():
        for _, copy in z_copies:
            copy.wait_recv()
        total = y_sum[rows_at(my_piece, piece), :]
        for k in range(zs - 1):
            total = total + z_parts[k]
        at = rows_at(my_part + my_piece, piece)
        new_modes_ref[at, :] = modes_ref[at, :] - rate * total

    gathers = []
    for k in range(1, zs):
        z, device = place.ring_z(k)
        ref = new_modes_ref.at[rows_at(my_part + my_piece, piece)]
        copy = remote(ref, ref, (zg_send, zg_recv), k - 1, device)
        pl.when(owner)(copy.start)
        gathers.append((owner, lax.rem(place.z + zs - k, zs) < owners, copy))
    for _, from_owner, copy in gathers:
        pl.when(from_owner)(copy.wait_recv)
    yg_copies = []
    for k in range(1, ys):
        ref = new_modes_ref.at[rows_at(my_part, part)]
        copy = remote(ref, ref, (yg_send, yg_recv), k - 1, place.ring_tile(k)[1])
        copy.start()
        yg_copies.append(copy)
    for copy in yg_copies:
        copy.wait_recv()
    xg_copies, cg_copies = [], []
    for k in range(1, xs):
        ref = new_modes_ref.at[rows_at(my_quarter, quarter)]
        copy = remote(ref, ref, (xg_send, xg_recv), k - 1, place.ring_x(k)[1])
        copy.start()
        xg_copies.append(copy)
    ref = new_modes_ref.at[rows_at(my_quarter, quarter)]
    copy = remote(ref, ref, (cg_send, cg_recv), 0, place.at_core())
    copy.start()
    cg_copies.append(copy)

    for copy in tile_copies:
        copy.wait_recv()
    total = strip[:, :, pl.ds(pl.multiple_of(place.tile * width, LANES), width)]
    for k in range(ys - 1):
        total = total + tile_parts[k]
    new_field_ref[...] = field_ref[...] - OBJECT_RATE * total

    for k, copy in zip(range(1, xs), xg_copies):
        copy.wait_recv()
        x = lax.rem(place.x + xs - k, xs)
        ref = new_modes_ref.at[rows_at(mine + x * quarter, quarter)]
        copy = remote(ref, ref, (cg_send, cg_recv), k, place.at_core())
        copy.start()
        cg_copies.append(copy)
    for copy in cg_copies:
        copy.wait()
    for copy in core_copies + x_copies + y_copies + tile_copies + yg_copies + xg_copies:
        copy.wait_send()
    for condition, copy in z_copies:
        pl.when(condition)(copy.wait_send)
    for condition, _, copy in gathers:
        pl.when(condition)(copy.wait_send)
    for exists, _, copy in sends:
        pl.when(exists)(copy.wait_send)


def reduce_gradients(columns, grad, grad_modes, field, modes, reach, chips_z, rate, collective_id):
    _, rows, width = field.shape
    slots, _, _, patch = grad.shape
    tiles, scans = lax.axis_size("tile"), lax.axis_size("scan")
    chips_x = scans // (CORES * chips_z)
    flat = (modes.size // patch, patch)
    half = flat[0] // CORES
    quarter = half // chips_x
    part = quarter // tiles
    owners = max(n for n in range(1, chips_z + 1) if part % (8 * n) == 0)
    piece = part // owners
    near = 2 * reach
    vmem = pl.BlockSpec(memory_space=pltpu.VMEM)
    f32 = functools.partial(pltpu.VMEM, dtype=jnp.float32)
    dma = pltpu.SemaphoreType.DMA
    counts = [near, tiles - 1, chips_x, chips_x - 1, tiles - 1, chips_z - 1, chips_z - 1, tiles - 1, chips_x - 1, chips_x]
    new_field, new_modes = pl.pallas_call(
        functools.partial(reduce_kernel, reach, chips_z, owners, rate),
        out_shape=(
            jax.ShapeDtypeStruct(field.shape, jnp.float32),
            jax.ShapeDtypeStruct(flat, jnp.float32),
        ),
        in_specs=[pl.BlockSpec(memory_space=pltpu.SMEM), vmem, vmem, vmem, vmem],
        out_specs=(vmem, vmem),
        scratch_shapes=[
            f32((near + 1, slots, 2, rows, patch)),
            f32((2, rows, width * tiles)),
            f32((tiles - 1, 2, rows, width)),
            f32((half, patch)),
            f32((half, patch)),
            f32((chips_x - 1, quarter, patch)),
            f32((quarter, patch)),
            f32((tiles - 1, part, patch)),
            f32((part, patch)),
            f32((chips_z - 1, piece, patch)),
        ]
        + [dma((n,)) for n in counts for _ in range(2)],
        compiler_params=pltpu.CompilerParams(
            collective_id=collective_id, has_side_effects=True, vmem_limit_bytes=VMEM_LIMIT
        ),
    )(columns, grad, grad_modes.reshape(flat), field, modes.reshape(flat))
    return new_field, new_modes.reshape(modes.shape)


def on_device(chips_z, object_field, probe, amplitude, positions, scan_list):
    tile_rows = object_field.shape[1]
    patch = probe.shape[2]
    reach = patch // (2 * tile_rows)
    total = positions.shape[0]
    slots = scan_list.shape[0]
    tables = jnp.asarray(dft_tables(patch))
    match = scan_list[:, None] == jnp.arange(total, dtype=jnp.int32)[None, :]
    found = jnp.sum(jnp.where(match[:, :, None], positions[None], 0), axis=1)
    row_start = found[:, 0] - lax.axis_index("scan") * tile_rows + patch // 2
    own_columns = jnp.zeros((8, LANES), jnp.int32).at[0, :slots].set(found[:, 1])
    field = object_field
    modes = probe
    columns = None
    for rounds in range(ITERATIONS):
        if rounds == 0:
            windows, table = gather_windows(field, own_columns, reach, slots, patch, chips_z, True, 1)
            columns = table[:, 0, :slots]
        else:
            windows = gather_windows(field, columns, reach, slots, patch, chips_z, False, 2)
        grad, grad_modes = slot_gradients(row_start, windows, modes, amplitude, tables)
        field, modes = reduce_gradients(
            columns, grad, grad_modes, field, modes, reach, chips_z, PROBE_RATE / total, 3
        )
    return (field, modes)


def solution(mesh, chips_z=CHIPS_Z):
    in_specs = (
        P(None, "scan", "tile"),
        P(),
        P(("scan", "tile"), None, None),
        P(),
        P(("scan", "tile")),
    )
    out_specs = (P(None, "scan", "tile"), P())
    return jax.shard_map(
        functools.partial(on_device, chips_z),
        mesh=mesh,
        in_specs=in_specs,
        out_specs=out_specs,
        check_vma=False,
    )
```

time: 946 us -> 208 us (0.22)
  waiting for transfers between devices: 547 us -> 0 us
  Pallas kernels: 0 us -> 200 us
  matrix products: 152 us -> 0 us
  starting transfers between devices: 95.8 us -> 0 us
  local copies, waits for them, and re-layouts: 57.8 us -> 5.27 us
  other arithmetic: 28.4 us -> 1.74 us
  blocking collectives: 22.3 us -> 0 us
  loops' own time: 21.9 us -> 0 us
  between operations: 16.1 us -> 0.73 us
    psum x2 -> x0, waiting for transfers between devices: 440 us -> none  [on_device(): grad_modes = lax.psum(grad_modes, ('scan', 'tile'))]
    pallas_call x0 -> x6, Pallas kernels: none -> 200 us  [the longest x2 118 us: reduce_gradients(): pl.pallas_call(functools.partial(reduce_kernel, reach, chips_z, owners, r...]
    dot_general x64 -> x0, matrix products: 152 us -> none  [the longest x32 76.7 us: apply_right(): jnp.einsum('mky,ly->mkl', values, table, precision=lax.Precision.HIGHEST)]
    ppermute x32 -> x0, starting transfers between devices: 95.6 us -> none  [shifted(): return lax.ppermute(block, axis, route)]
    ppermute x32 -> x0, waiting for transfers between devices: 83.2 us -> none  [shifted(): return lax.ppermute(block, axis, route)]
    dynamic_update_slice x4 -> x0, local copies, waits for them, and re-layouts: 24.2 us -> none  [visit(): lax.dynamic_update_slice(grad_band, previous + jnp.stack([term_real, term...]
    reduce_scatter x2 -> x0, waiting for transfers between devices: 22.5 us -> none  [on_device(): lax.psum_scatter(disperse(grad_band, reach, tile_rows), 'tile', scatter_d...]
    all_gather x2 -> x0, blocking collectives: 22.3 us -> none  [on_device(): band = assemble(lax.all_gather(field, 'tile', axis=2, tiled=True), reach)]
  transfers between devices with their start and end apart: 36 -> 0, of which waited for: 17 -> 0; matrix products, arithmetic and copies ran while one was open for 2% -> 0% of each run, Pallas kernels for 0% -> 0%
where the time goes in v1:
time: 208 us
  Pallas kernels  200 us (96%)
  local copies, waits for them, and re-layouts  5.27 us (3%)
    pallas_call x2, Pallas kernels, reduce_gradients(): pl.pallas_call(functools.partial(reduce_kernel, reach, chips_z, owners, r...  118 us
    pallas_call x2, Pallas kernels, gather_windows(): pl.pallas_call(functools.partial(gather_kernel, reach, chips_z, exchange)...  49.3 us
    pallas_call x2, Pallas kernels, slot_gradients(): pl.pallas_call(slots_kernel, out_shape=(jax.ShapeDtypeStruct(windows.shap...  32.3 us
    unnamed x12, local copies, waits for them, and re-layouts  5.07 us

profile of v1, /device:TPU:1, one launch (start us, length us, event | category | flops | bytes accessed | tf_op | source)
XLA Modules:
  0.0 207.6 jit_solution(10798451110017078492)
XLA Ops:
  0.6 0.7 iota_compare_fusion
  1.4 0.8 select_reduce_fusion
  2.2 0.2 add_reduce_fusion
  2.4 0.0 copy-start.2
  2.4 0.8 copy-done.2
  3.2 27.0 %shard_map.77 = (f32[2,2,288,256]{3,2,1,0:T(8,128)S(1)}, s32[9,8,128]{2,1,0:T(8,128)S(1)}) custom-call(f32[2,32,256]{2,1,0:T(8,128)S(1)} %copy-done.2, s32[8,128]{1,0:T(8,128)S(1)} %scatter.4.refs_1_), custom_call_target="tpu_custom_call" | custom-call | tf_op jit(solution)/shard_map/pallas_call | solution.py:334
  30.3 0.1 copy.17
  30.4 0.1 copy.20.columns.refs_1_
  30.5 0.0 copy-start
  30.5 1.4 copy-done
  31.9 0.0 copy-start.4
  31.9 1.0 copy-done.4
  32.9 0.0 copy-start.1
  32.9 0.0 copy-start.3
  32.9 16.3 %shard_map.78 = (f32[2,2,288,256]{3,2,1,0:T(8,128)S(1)}, f32[2,3,256,256]{3,2,1,0:T(8,128)S(1)}) custom-call(s32[2]{0:T(128)S(1)} %get-tuple-element.34.rows_ref, f32[2,2,288,256]{3,2,1,0:T(8,128)S(1)} %get-tuple-element.25.window_ref, f32[2,3,256,256]{3,2,1,0:T(8,128)S(1)} %copy-done, f32[2,256,256]{2,1,0:T(8,128)S(1)} %copy-done.4, ...), custom_call_target="tpu_custom_call" | custom-call | flops 9663676416 | bytes 6029312 | tf_op jit(solution)/shard_map/pallas_call | solution.py:134
  49.2 0.0 copy-done.1
  49.2 0.0 copy-done.3
  49.2 59.6 %shard_map.79 = (f32[2,32,256]{2,1,0:T(8,128)S(1)}, f32[1536,256]{1,0:T(8,128)S(1)}) custom-call(s32[9,2]{1,0:T(8,128)S(1)} %copy.20.columns.refs_1_, f32[2,2,288,256]{3,2,1,0:T(8,128)S(1)} %get-tuple-element.26.grad_ref, f32[1536,256]{1,0:T(8,128)S(1)} %bitcast.11, f32[2,32,256]{2,1,0:T(8,128)S(1)} %copy-done.3, f32[1536,256]{1,0:T(8,128)S(1)} %bitcast.7), custom_call_target="tpu_custom_call" | custom-call | tf_op jit(solution)/shard_map/pallas_call | solution.py:563
  108.8 22.2 %shard_map.80.window_ref = f32[2,2,288,256]{3,2,1,0:T(8,128)S(1)} custom-call(f32[2,32,256]{2,1,0:T(8,128)S(1)} %get-tuple-element.28.refs_0_.field_ref, s32[9,2]{1,0:T(8,128)S(1)} %copy.20.columns.refs_1_), custom_call_target="tpu_custom_call" | custom-call | tf_op jit(solution)/shard_map/pallas_call | solution.py:334
  131.1 16.1 %shard_map.81 = (f32[2,2,288,256]{3,2,1,0:T(8,128)S(1)}, f32[2,3,256,256]{3,2,1,0:T(8,128)S(1)}) custom-call(s32[2]{0:T(128)S(1)} %get-tuple-element.34.rows_ref, f32[2,2,288,256]{3,2,1,0:T(8,128)S(1)} %shard_map.80.window_ref, f32[2,3,256,256]{3,2,1,0:T(8,128)S(1)} %bitcast.8, f32[2,256,256]{2,1,0:T(8,128)S(1)} %copy-done.4, ...), custom_call_target="tpu_custom_call" | custom-call | flops 9663676416 | bytes 6029312 | tf_op jit(solution)/shard_map/pallas_call | solution.py:134
  147.1 58.7 %shard_map.82 = (f32[2,32,256]{2,1,0:T(8,128)S(1)}, f32[1536,256]{1,0:T(8,128)S(1)}) custom-call(s32[9,2]{1,0:T(8,128)S(1)} %copy.20.columns.refs_1_, f32[2,2,288,256]{3,2,1,0:T(8,128)S(1)} %get-tuple-element.30.grad_ref, f32[1536,256]{1,0:T(8,128)S(1)} %bitcast.9, f32[2,32,256]{2,1,0:T(8,128)S(1)} %get-tuple-element.28.refs_0_.field_ref, ...), custom_call_target="tpu_custom_call" | custom-call | tf_op jit(solution)/shard_map/pallas_call | solution.py:563
  205.8 0.6 copy.23
  206.4 1.1 copy.24
  (2 shorter events, 0.0 us)
Async XLA Ops:
  2.4 0.8 copy-start.2
  30.5 1.4 copy-start
  31.9 1.0 copy-start.4
  32.9 16.3 %copy-start.1 = (f32[2,3,256,256]{3,2,1,0:T(8,128)S(1)}, f32[2,3,256,256]{3,2,1,0:T(8,128)}, u32[]{:S(2)}) copy-start(f32[2,3,256,256]{3,2,1,0:T(8,128)} %modes_ref.1) | copy-start | bytes 4718596
  32.9 16.3 %copy-start.3 = (f32[2,32,256]{2,1,0:T(8,128)S(1)}, f32[2,32,256]{2,1,0:T(8,128)}, u32[]{:S(2)}) copy-start(f32[2,32,256]{2,1,0:T(8,128)} %field_ref.1) | copy-start | bytes 196612

commit v2 on v0

v2 whole, which is shorter than its diff:
```python
import functools
import math

import jax
import jax.numpy as jnp
import ml_dtypes
import numpy as np
from jax import lax
from jax.experimental import pallas as pl
from jax.experimental.pallas import tpu as pltpu
from jax.sharding import PartitionSpec as P

ITERATIONS = 2
INTENSITY_FLOOR = 0.1
OBJECT_RATE = 0.05
PROBE_RATE = 0.5

CORES = 2
CHIPS_Z = 8
LANES = 128
MESH = pl.DeviceIdType.MESH
VMEM_LIMIT = 56 * 1024 * 1024


def dft_tables(length):
    index = np.arange(length // 2)
    scale = 1.0 / math.sqrt(length)
    tables = []
    for parity in range(2):
        phase = np.outer(index, 2 * index + parity) % length
        angle = phase * (-2.0 * math.pi / length)
        cosine, sine = np.cos(angle) * scale, np.sin(angle) * scale
        forward = np.block([[cosine, sine], [-sine, cosine]])
        for table in (forward, forward.T):
            high = table.astype(ml_dtypes.bfloat16)
            low = (table - high.astype(np.float64)).astype(ml_dtypes.bfloat16)
            tables += [high, low]
    order = np.concatenate([np.arange(0, length, 2), np.arange(1, length, 2)])
    tables.append(np.eye(length)[:, order].astype(ml_dtypes.bfloat16))
    return np.stack(tables)


def halves(values):
    high = values.astype(jnp.bfloat16)
    low = (values - high.astype(jnp.float32)).astype(jnp.bfloat16)
    return high, low


def product(left, right):
    dot = functools.partial(jnp.dot, preferred_element_type=jnp.float32)
    return dot(left[0], right[0]) + (dot(left[0], right[1]) + dot(left[1], right[0]))


def permuted(values, order):
    total = None
    for _ in range(3):
        part = values.astype(jnp.bfloat16)
        values = values - part.astype(jnp.float32)
        moved = jnp.dot(part, order, preferred_element_type=jnp.float32)
        total = moved if total is None else total + moved
    return total


def beside(parts):
    return jnp.concatenate(parts, axis=1)


def stacked(parts):
    return jnp.concatenate(parts, axis=0)


class Place:
    def __init__(self, chips_z):
        self.scan = lax.axis_index("scan")
        self.tile = lax.axis_index("tile")
        self.scans = lax.axis_size("scan")
        self.tiles = lax.axis_size("tile")
        self.chips_z = chips_z
        self.chips_x = self.scans // (chips_z * CORES)
        self.core = lax.rem(self.scan, CORES)
        self.z = lax.rem(self.scan // CORES, chips_z)
        self.x = self.scan // (CORES * chips_z)

    def at_core(self):
        return (self.scan + 1 - 2 * self.core, self.tile)

    def ring_x(self, k):
        x = lax.rem(self.x + k, self.chips_x)
        return x, ((x * self.chips_z + self.z) * CORES + self.core, self.tile)

    def ring_z(self, k):
        z = lax.rem(self.z + k, self.chips_z)
        return z, ((self.x * self.chips_z + z) * CORES + self.core, self.tile)

    def ring(self, axis, k):
        return self.ring_x(k) if axis == "x" else self.ring_tile(k)

    def along(self, axis):
        return (self.x, self.chips_x) if axis == "x" else (self.tile, self.tiles)

    def ring_tile(self, k):
        tile = lax.rem(self.tile + k, self.tiles)
        return tile, (self.scan, tile)

    def near(self, d):
        other = self.scan + d
        return jnp.logical_and(other >= 0, other < self.scans), (other, self.tile)


def distances(reach):
    far_first = sorted(range(1, reach + 1), reverse=True)
    return [sign * d for d in far_first for sign in (1, -1)]


def greet(partners):
    barrier = pltpu.get_barrier_semaphore()
    total = 0
    for condition, device in partners:
        if condition is None:
            pl.semaphore_signal(barrier, inc=1, device_id=device, device_id_type=MESH)
            total = total + 1
        else:

            @pl.when(condition)
            def _(device=device):
                pl.semaphore_signal(barrier, inc=1, device_id=device, device_id_type=MESH)

            total = total + condition.astype(jnp.int32)
    pl.semaphore_wait(barrier, total)


def sublane(shape):
    return lax.broadcasted_iota(jnp.int32, shape, 1)


def read_patch(band, row, patch):
    groups, margin = patch // 8, (band.shape[0] - patch) // 8
    tiled = band.reshape(groups + margin, 8, band.shape[1])
    block, inside = row // 8, lax.rem(row, 8)
    values = tiled[: groups + 1]
    for q in range(1, margin):
        values = jnp.where(block == q, tiled[q : q + groups + 1], values)
    turned = pltpu.roll(values, lax.rem(8 - inside, 8), 1)
    values = jnp.where(sublane(turned[1:].shape) < 8 - inside, turned[:-1], turned[1:])
    return values.reshape(patch, band.shape[1])


def place_patch(values, row, margin):
    patch, width = values.shape
    groups, margin = patch // 8, margin // 8
    block, inside = row // 8, lax.rem(row, 8)
    turned = pltpu.roll(values.reshape(groups, 8, width), inside, 1)
    edge = jnp.zeros((1, 8, width), values.dtype)
    before = stacked([edge, turned])
    after = stacked([turned, edge])
    values = jnp.where(sublane(before.shape) < inside, before, after)
    pad = jnp.zeros((margin - 1, 8, width), values.dtype)
    padded = stacked([pad, values, pad])
    band = padded[margin - 1 :]
    for q in range(1, margin):
        start = margin - 1 - q
        band = jnp.where(block == q, padded[start : start + groups + margin], band)
    return band.reshape((groups + margin) * 8, width)


def slot_gradient(row, window, modes, amplitude, tables, grad, grad_modes, patch_ref, pattern_ref, slot):
    patch = patch_ref.shape[1]
    count = modes.shape[0] // (2 * patch)
    half = patch // 2
    straight = [(tables[4 * p], tables[4 * p + 1]) for p in range(2)]
    turned = [(tables[4 * p + 2], tables[4 * p + 3]) for p in range(2)]

    def rows_of(part, m):
        return slice((part * count + m) * patch, (part * count + m + 1) * patch)

    for part in range(2):
        patch_ref[part] = read_patch(window[part], row, patch)
    pieces = [[], []]
    for m in range(count):
        patch_real, patch_imag = patch_ref[0], patch_ref[1]
        mode_real, mode_imag = modes[rows_of(0, m), :], modes[rows_of(1, m), :]
        real = mode_real * patch_real - mode_imag * patch_imag
        imag = mode_real * patch_imag + mode_imag * patch_real
        pieces[0].append(beside([real[:, :half] + real[:, half:], imag[:, :half] + imag[:, half:]]))
        pieces[1].append(beside([real[:, :half] - real[:, half:], imag[:, :half] - imag[:, half:]]))
    columns = [product(halves(stacked(pieces[p])), straight[p]) for p in range(2)]
    far = [[], []]
    power = [None, None]
    for m in range(count):
        even, odd = (columns[p][m * patch : (m + 1) * patch] for p in range(2))
        real = beside([even[:, :half], odd[:, :half]])
        imag = beside([even[:, half:], odd[:, half:]])
        pieces = (
            stacked([real[:half] + real[half:], imag[:half] + imag[half:]]),
            stacked([real[:half] - real[half:], imag[:half] - imag[half:]]),
        )
        for p in range(2):
            value = product(turned[p], halves(pieces[p]))
            far[p].append(value)
            square = value[:half] * value[:half] + value[half:] * value[half:]
            power[p] = square if power[p] is None else power[p] + square
    pattern = permuted(amplitude[...], tables[8])
    pattern_ref[0] = pattern[:, :half]
    pattern_ref[1] = pattern[:, half:]
    factor = []
    for p in range(2):
        pattern = beside([pattern_ref[q, pl.ds(p, half, stride=2), :] for q in range(2)])
        value = 1.0 - pattern * lax.rsqrt(jnp.maximum(power[p], INTENSITY_FLOOR))
        factor.append(stacked([value, value]))
    pieces = [[], []]
    for m in range(count):
        even, odd = (product(straight[p], halves(far[p][m] * factor[p])) for p in range(2))
        upper, lower = even + odd, even - odd
        real = stacked([upper[:half], lower[:half]])
        imag = stacked([upper[half:], lower[half:]])
        pieces[0].append(beside([real[:, :half], imag[:, :half]]))
        pieces[1].append(beside([real[:, half:], imag[:, half:]]))
    columns = [product(halves(stacked(pieces[p])), turned[p]) for p in range(2)]
    term_real = term_imag = None
    for m in range(count):
        even, odd = (columns[p][m * patch : (m + 1) * patch] for p in range(2))
        upper, lower = even + odd, even - odd
        back_real = beside([upper[:, :half], lower[:, :half]])
        back_imag = beside([upper[:, half:], lower[:, half:]])
        patch_real, patch_imag = patch_ref[0], patch_ref[1]
        mode_real, mode_imag = modes[rows_of(0, m), :], modes[rows_of(1, m), :]
        real = mode_real * back_real + mode_imag * back_imag
        imag = mode_real * back_imag - mode_imag * back_real
        term_real = real if term_real is None else term_real + real
        term_imag = imag if term_imag is None else term_imag + imag
        probe_real = patch_real * back_real + patch_imag * back_imag
        probe_imag = patch_real * back_imag - patch_imag * back_real
        if slot == 0:
            grad_modes[rows_of(0, m), :] = probe_real
            grad_modes[rows_of(1, m), :] = probe_imag
        else:
            grad_modes[rows_of(0, m), :] += probe_real
            grad_modes[rows_of(1, m), :] += probe_imag
    margin = window.shape[1] - patch
    grad[0] = place_patch(term_real, row, margin)
    grad[1] = place_patch(term_imag, row, margin)


def rows_at(start, size):
    return pl.ds(pl.multiple_of(start, 8), size)


def iterations_kernel(names, reach, chips_z, owners, rate, *refs):
    at_name = dict(zip(names, refs))
    first_field, first_modes = at_name["field"], at_name["modes"]
    rows_ref, amplitude, tables = at_name["rows"], at_name["amplitude"], at_name["tables"]
    columns, table = at_name["columns"], at_name["table"]
    place = Place(chips_z)
    _, rows, width = first_field.shape
    slots, patch = amplitude.shape[0], amplitude.shape[1]
    order = distances(reach)
    xs, ys, zs = place.chips_x, place.tiles, place.chips_z
    half = first_modes.shape[0] // CORES
    chains = (("x", "tile"), ("tile", "x"))
    chain = half // len(chains)
    part = chain // (xs * ys)
    piece = part // owners
    lane = lax.broadcasted_iota(jnp.int32, (rows, LANES), 1)
    blocks = width * ys // LANES
    wide = width // LANES
    finish = []

    def sems(name, *index):
        return at_name[name + "_send"].at[index], at_name[name + "_recv"].at[index]

    def copy_to(src, dst, device, name, *index):
        send, recv = sems(name, *index)
        return pltpu.make_async_remote_copy(
            src_ref=src, dst_ref=dst, send_sem=send, recv_sem=recv, device_id=device, device_id_type=MESH
        )

    def send(copy, condition=None):
        if condition is None:
            copy.start()
            finish.append(copy.wait_send)
        else:
            pl.when(condition)(copy.start)
            finish.append(lambda: pl.when(condition)(copy.wait_send))

    def owns(chain_at, z):
        return lax.rem(z + zs * len(chains) - chain_at * owners, zs)

    partners = [(None, place.at_core())]
    partners += [(None, place.ring_x(k)[1]) for k in range(1, xs)]
    partners += [(None, place.ring_tile(k)[1]) for k in range(1, ys)]
    for k in range(1, zs):
        z, device = place.ring_z(k)
        meets = functools.reduce(
            jnp.logical_or, [owns(c, at) < owners for c in range(len(chains)) for at in (z, place.z)]
        )
        partners.append((meets, device))
    partners += [place.near(d) for d in order]
    greet(partners)

    def share_strip(it, field):
        strip = at_name["strip"].at[it]
        own = pl.ds(pl.multiple_of(place.tile * width, LANES), width)
        copies = []
        for k in range(1, ys):
            copy = copy_to(field, strip.at[:, :, own], place.ring_tile(k)[1], "strip", it, k - 1)
            send(copy)
            copies.append(copy)
        strip[:, :, own] = field[...]
        return copies

    def cut(it, source, slot, target):
        strip = at_name["strip"].at[it]
        column = columns[source, 0, slot]
        first = column // LANES
        inside = column - first * LANES
        for p in range(2):
            pieces = []
            for i in range(wide + 1):
                value = strip[p, :, LANES * i : LANES * (i + 1)]
                for block in range(1, blocks - wide + 1):
                    at = min(block + i, blocks - 1)
                    value = jnp.where(first == block, strip[p, :, LANES * at : LANES * (at + 1)], value)
                pieces.append(pltpu.roll(value, lax.rem(LANES - inside, LANES), 1))
            for i in range(wide):
                target[p, :, LANES * i : LANES * (i + 1)] = jnp.where(
                    lane < LANES - inside, pieces[i], pieces[i + 1]
                )

    def send_windows(it, slot):
        window = at_name["window"].at[it, slot]
        copies = []
        for at, d in enumerate(order):
            exists, device = place.near(d)
            outgoing = at_name["outgoing"].at[it, slot, at]
            copy = copy_to(
                outgoing, window.at[:, (reach - d) * rows : (reach - d + 1) * rows, :],
                device, "window", it, slot, at,
            )
            cut(it, reach + d, slot, outgoing)
            send(copy, exists)
            copies.append((place.near(-d)[0], copy))
        cut(it, reach, slot, window.at[:, reach * rows : (reach + 1) * rows, :])
        return copies

    def send_gradient(it, slot):
        grad = at_name["grad"].at[it, slot]
        arrived = at_name["arrived"].at[it, slot]
        copies = []
        for at, d in enumerate(order):
            exists, device = place.near(d)
            copy = copy_to(
                grad.at[:, (reach + d) * rows : (reach + d + 1) * rows, :], arrived.at[reach - d],
                device, "grad", it, slot, at,
            )
            send(copy, exists)
            copies.append((place.near(-d)[0], copy))
        arrived[reach] = grad[:, reach * rows : (reach + 1) * rows, :]
        return copies

    def place_windows(it, slot):
        strip = at_name["grad_strip"].at[it]
        arrived = at_name["arrived"].at[it, slot]

        def place_window(source, carry):
            column = columns[source, 0, slot]
            first = column // LANES
            inside = column - first * LANES
            for p in range(2):
                values = [
                    pltpu.roll(arrived[source, p, :, LANES * i : LANES * (i + 1)], inside, 1)
                    for i in range(wide)
                ]
                values = [jnp.zeros_like(values[0])] + values + [jnp.zeros_like(values[0])]
                shifted = [jnp.where(lane < inside, values[i], values[i + 1]) for i in range(wide + 1)]
                for block in range(blocks):
                    term = jnp.zeros_like(values[0])
                    for i, value in enumerate(shifted):
                        term = jnp.where(first + i == block, value, term)
                    strip[p, :, LANES * block : LANES * (block + 1)] += term
            return carry

        lax.fori_loop(0, 2 * reach + 1, place_window, 0)

    def wait_near(copies):
        for exists, copy in copies:
            pl.when(exists)(copy.wait_recv)

    strip_copies = share_strip(0, first_field)
    table[reach] = at_name["own_columns"][...]
    notes = []
    for at, d in enumerate(order):
        exists, device = place.near(d)
        copy = copy_to(at_name["own_columns"], table.at[reach - d], device, "note", at)
        send(copy, exists)
        notes.append((place.near(-d)[0], copy))
    for d in order:

        @pl.when(jnp.logical_not(place.near(-d)[0]))
        def _(d=d):
            table[reach - d] = jnp.zeros(table.shape[1:], jnp.int32)
            for it in range(ITERATIONS):
                for slot in range(slots):
                    at_name["window"][it, slot, :, (reach - d) * rows : (reach - d + 1) * rows, :] = (
                        jnp.zeros((2, rows, patch), jnp.float32)
                    )
                    at_name["arrived"][it, slot, reach - d] = jnp.zeros((2, rows, patch), jnp.float32)

    at_name["grad_strip"][...] = jnp.zeros(at_name["grad_strip"].shape, jnp.float32)
    wait_near(notes)
    local = pltpu.make_async_copy(table, columns, at_name["local"])
    local.start()
    local.wait()
    for copy in strip_copies:
        copy.wait_recv()
    window_copies = [send_windows(0, slot) for slot in range(slots)]

    for it in range(ITERATIONS):
        last = it == ITERATIONS - 1
        field = first_field if it == 0 else at_name["field_between"]
        modes = first_modes if it == 0 else at_name["modes_between"]
        new_field = at_name["new_field"] if last else at_name["field_between"]
        new_modes = at_name["new_modes"] if last else at_name["modes_between"]
        grad_modes = at_name["grad_modes"].at[it]

        grad_copies = []
        for slot in range(slots):
            wait_near(window_copies[slot])
            slot_gradient(
                rows_ref[slot], at_name["window"].at[it, slot], modes, amplitude.at[slot], tables,
                at_name["grad"].at[it, slot], grad_modes, at_name["patch"], at_name["pattern"], slot,
            )
            if slot < slots - 1:
                grad_copies.append(send_gradient(it, slot))

        mine, other = place.core * half, (1 - place.core) * half
        core_part, core_sum = at_name["core_part"].at[it], at_name["core_sum"].at[it]
        core_copies = []
        for k in range(1, max(xs, ys) + 1):
            for c, (axis, _) in enumerate(chains):
                here, size = place.along(axis)
                if k > size:
                    continue
                quarter = chain // size
                start = c * chain + lax.rem(here + k, size) * quarter
                copy = copy_to(
                    grad_modes.at[rows_at(other + start, quarter)], core_part.at[rows_at(start, quarter)],
                    place.at_core(), "core", it, c, k - 1,
                )
                send(copy)
                core_copies.append((c, axis, k, size, quarter, start, copy))
        grad_copies.append(send_gradient(it, slots - 1))
        one_copies = [[], []]
        for c, axis, k, size, quarter, start, copy in core_copies:
            copy.wait_recv()
            at = rows_at(start, quarter)
            core_sum[at, :] = core_part[at, :] + grad_modes[rows_at(mine + start, quarter), :]
            if k < size:
                copy = copy_to(
                    core_sum.at[at], at_name["one_parts"].at[it, c, k - 1, pl.ds(0, quarter)],
                    place.ring(axis, k)[1], "one", it, c, k - 1,
                )
                send(copy)
                one_copies[c].append(copy)
        for slot in range(slots - 1):
            wait_near(grad_copies[slot])
            place_windows(it, slot)
        two_copies = [[], []]
        for c, (axis, axis_two) in enumerate(chains):
            here, size = place.along(axis)
            quarter = chain // size
            for copy in one_copies[c]:
                copy.wait_recv()
            total = core_sum[rows_at(c * chain + here * quarter, quarter), :]
            for k in range(size - 1):
                total = total + at_name["one_parts"][it, c, k, :quarter, :]
            one_sum = at_name["one_sum"].at[it, c, pl.ds(0, quarter)]
            one_sum[...] = total
            for k in range(1, place.along(axis_two)[1]):
                to, device = place.ring(axis_two, k)
                copy = copy_to(
                    one_sum.at[rows_at(to * part, part)], at_name["two_parts"].at[it, c, k - 1],
                    device, "two", it, c, k - 1,
                )
                send(copy)
                two_copies[c].append(copy)

        wait_near(grad_copies[slots - 1])
        place_windows(it, slots - 1)
        grad_strip = at_name["grad_strip"].at[it]
        tile_copies = []
        for k in range(1, ys):
            y, device = place.ring_tile(k)
            copy = copy_to(
                grad_strip.at[:, :, pl.ds(pl.multiple_of(y * width, LANES), width)],
                at_name["tile_parts"].at[it, k - 1], device, "tile", it, k - 1,
            )
            send(copy)
            tile_copies.append(copy)

        z_copies = [[], []]
        for c, (_, axis_two) in enumerate(chains):
            here, size = place.along(axis_two)
            for copy in two_copies[c]:
                copy.wait_recv()
            total = at_name["one_sum"][it, c, rows_at(here * part, part), :]
            for k in range(size - 1):
                total = total + at_name["two_parts"][it, c, k]
            two_sum = at_name["two_sum"].at[it, c]
            two_sum[...] = total
            for k in range(1, zs):
                z, device = place.ring_z(k)
                owned = owns(c, z)
                copy = copy_to(
                    two_sum.at[rows_at(jnp.minimum(owned, owners - 1) * piece, piece)],
                    at_name["z_parts"].at[it, c, k - 1], device, "z", it, c, k - 1,
                )
                send(copy, owned < owners)
                z_copies[c].append(copy)

        for copy in tile_copies:
            copy.wait_recv()
        total = grad_strip[:, :, pl.ds(pl.multiple_of(place.tile * width, LANES), width)]
        for k in range(ys - 1):
            total = total + at_name["tile_parts"][it, k]
        new_field[...] = field[...] - OBJECT_RATE * total
        if not last:
            strip_copies = share_strip(it + 1, new_field)

        my_quarters, my_parts, zg_copies = [], [], [[], []]
        for c, (axis, axis_two) in enumerate(chains):
            here, size = place.along(axis)
            my_quarter = mine + c * chain + here * (chain // size)
            my_part = my_quarter + place.along(axis_two)[0] * part
            my_quarters.append(my_quarter)
            my_parts.append(my_part)
            owned = owns(c, place.z)
            owner = owned < owners
            my_piece = jnp.minimum(owned, owners - 1) * piece

            @pl.when(owner)
            def _(c=c, my_part=my_part, my_piece=my_piece):
                for copy in z_copies[c]:
                    copy.wait_recv()
                total = at_name["two_sum"][it, c, rows_at(my_piece, piece), :]
                for k in range(zs - 1):
                    total = total + at_name["z_parts"][it, c, k]
                at = rows_at(my_part + my_piece, piece)
                new_modes[at, :] = modes[at, :] - rate * total

            for k in range(1, zs):
                ref = new_modes.at[rows_at(my_part + my_piece, piece)]
                copy = copy_to(ref, ref, place.ring_z(k)[1], "zg", it, c, k - 1)
                send(copy, owner)
                zg_copies[c].append((owns(c, lax.rem(place.z + zs - k, zs)) < owners, copy))
        two_copies = [[], []]
        for c, (_, axis_two) in enumerate(chains):
            wait_near(zg_copies[c])
            for k in range(1, place.along(axis_two)[1]):
                ref = new_modes.at[rows_at(my_parts[c], part)]
                copy = copy_to(ref, ref, place.ring(axis_two, k)[1], "twog", it, c, k - 1)
                send(copy)
                two_copies[c].append(copy)
        if not last:
            for copy in strip_copies:
                copy.wait_recv()
            window_copies = [send_windows(it + 1, slot) for slot in range(slots)]
        one_copies, core_copies = [[], []], []
        for c, (axis, _) in enumerate(chains):
            for copy in two_copies[c]:
                copy.wait_recv()
            here, size = place.along(axis)
            quarter = chain // size
            ref = new_modes.at[rows_at(my_quarters[c], quarter)]
            for k in range(1, size):
                copy = copy_to(ref, ref, place.ring(axis, k)[1], "oneg", it, c, k - 1)
                send(copy)
                one_copies[c].append(copy)
            copy = copy_to(ref, ref, place.at_core(), "coreg", it, c, 0)
            send(copy)
            core_copies.append(copy)
        for k in range(1, max(xs, ys)):
            for c, (axis, _) in enumerate(chains):
                here, size = place.along(axis)
                if k >= size:
                    continue
                one_copies[c][k - 1].wait_recv()
                quarter = chain // size
                start = mine + c * chain + lax.rem(here + size - k, size) * quarter
                ref = new_modes.at[rows_at(start, quarter)]
                copy = copy_to(ref, ref, place.at_core(), "coreg", it, c, k)
                send(copy)
                core_copies.append(copy)
        for copy in core_copies:
            copy.wait_recv()
    for wait in finish:
        wait()


def on_device(chips_z, object_field, probe, amplitude, positions, scan_list):
    _, rows, width = object_field.shape
    patch = probe.shape[2]
    reach = patch // (2 * rows)
    near = 2 * reach
    total = positions.shape[0]
    slots = scan_list.shape[0]
    tiles, scans = lax.axis_size("tile"), lax.axis_size("scan")
    chips_x = scans // (CORES * chips_z)
    flat = (probe.size // patch, patch)
    half = flat[0] // CORES
    chain = half // 2
    part = chain // (chips_x * tiles)
    owners = max(n for n in range(1, chips_z + 1) if part % (8 * n) == 0)
    piece = part // owners
    longest = max(chips_x, tiles)
    quarter = chain // min(chips_x, tiles)

    tables = jnp.asarray(dft_tables(patch))
    match = scan_list[:, None] == jnp.arange(total, dtype=jnp.int32)[None, :]
    found = jnp.sum(jnp.where(match[:, :, None], positions[None], 0), axis=1)
    row_start = found[:, 0] - lax.axis_index("scan") * rows + patch // 2
    own_columns = jnp.zeros((8, LANES), jnp.int32).at[0, :slots].set(found[:, 1])

    def vmem(*shape):
        return pltpu.VMEM((ITERATIONS,) + shape, jnp.float32)

    band = (2, (near + 1) * rows, patch)
    block = (2, rows, patch)
    scratch = {
        "columns": pltpu.SMEM((near + 1, 8, LANES), jnp.int32),
        "table": pltpu.VMEM((near + 1, 8, LANES), jnp.int32),
        "strip": vmem(2, rows, width * tiles),
        "outgoing": vmem(slots, near, *block),
        "window": vmem(slots, *band),
        "grad": vmem(slots, *band),
        "arrived": vmem(slots, near + 1, *block),
        "grad_strip": vmem(2, rows, width * tiles),
        "tile_parts": vmem(tiles - 1, 2, rows, width),
        "field_between": pltpu.VMEM(object_field.shape, jnp.float32),
        "modes_between": pltpu.VMEM(flat, jnp.float32),
        "patch": pltpu.VMEM((2, patch, patch), jnp.float32),
        "pattern": pltpu.VMEM((2, patch, patch // 2), jnp.float32),
        "grad_modes": vmem(*flat),
        "core_part": vmem(half, patch),
        "core_sum": vmem(half, patch),
        "one_parts": vmem(2, longest - 1, quarter, patch),
        "one_sum": vmem(2, quarter, patch),
        "two_parts": vmem(2, longest - 1, part, patch),
        "two_sum": vmem(2, part, patch),
        "z_parts": vmem(2, chips_z - 1, piece, patch),
        "local": pltpu.SemaphoreType.DMA(()),
    }
    counts = {
        "note": (near,),
        "strip": (ITERATIONS, tiles - 1),
        "window": (ITERATIONS, slots, near),
        "grad": (ITERATIONS, slots, near),
        "tile": (ITERATIONS, tiles - 1),
        "core": (ITERATIONS, 2, longest),
        "one": (ITERATIONS, 2, longest - 1),
        "two": (ITERATIONS, 2, longest - 1),
        "z": (ITERATIONS, 2, chips_z - 1),
        "zg": (ITERATIONS, 2, chips_z - 1),
        "twog": (ITERATIONS, 2, longest - 1),
        "oneg": (ITERATIONS, 2, longest - 1),
        "coreg": (ITERATIONS, 2, longest),
    }
    for name, shape in counts.items():
        scratch[name + "_send"] = pltpu.SemaphoreType.DMA(shape)
        scratch[name + "_recv"] = pltpu.SemaphoreType.DMA(shape)
    inputs = ["rows", "own_columns", "field", "modes", "amplitude", "tables"]
    outputs = ["new_field", "new_modes"]
    names = inputs + outputs + list(scratch)
    in_vmem = pl.BlockSpec(memory_space=pltpu.VMEM)
    field, modes = pl.pallas_call(
        functools.partial(iterations_kernel, names, reach, chips_z, owners, PROBE_RATE / total),
        out_shape=(
            jax.ShapeDtypeStruct(object_field.shape, jnp.float32),
            jax.ShapeDtypeStruct(flat, jnp.float32),
        ),
        in_specs=[pl.BlockSpec(memory_space=pltpu.SMEM)] + [in_vmem] * 5,
        out_specs=(in_vmem, in_vmem),
        scratch_shapes=list(scratch.values()),
        compiler_params=pltpu.CompilerParams(
            collective_id=1, has_side_effects=True, vmem_limit_bytes=VMEM_LIMIT
        ),
    )(row_start, own_columns, object_field, probe.reshape(flat), amplitude, tables)
    return field, modes.reshape(probe.shape)


def solution(mesh, chips_z=CHIPS_Z):
    in_specs = (
        P(None, "scan", "tile"),
        P(),
        P(("scan", "tile"), None, None),
        P(),
        P(("scan", "tile")),
    )
    out_specs = (P(None, "scan", "tile"), P())
    return jax.shard_map(
        functools.partial(on_device, chips_z),
        mesh=mesh,
        in_specs=in_specs,
        out_specs=out_specs,
        check_vma=False,
    )
```

time: 946 us -> 143 us (0.15)
  waiting for transfers between devices: 547 us -> 0 us
  matrix products: 152 us -> 0 us
  Pallas kernels: 0 us -> 135 us
  starting transfers between devices: 95.8 us -> 0 us
  local copies, waits for them, and re-layouts: 57.8 us -> 4.81 us
  other arithmetic: 28.4 us -> 2.21 us
  blocking collectives: 22.3 us -> 0 us
  loops' own time: 21.9 us -> 0 us
  between operations: 16.1 us -> 0.65 us
    psum x2 -> x0, waiting for transfers between devices: 440 us -> none  [on_device(): grad_modes = lax.psum(grad_modes, ('scan', 'tile'))]
    dot_general x64 -> x0, matrix products: 152 us -> none  [the longest x32 76.7 us: apply_right(): jnp.einsum('mky,ly->mkl', values, table, precision=lax.Precision.HIGHEST)]
    pallas_call x0 -> x1, Pallas kernels: none -> 135 us  [on_device(): pl.pallas_call(functools.partial(iterations_kernel, names, reach, chips_z...]
    ppermute x32 -> x0, starting transfers between devices: 95.6 us -> none  [shifted(): return lax.ppermute(block, axis, route)]
    ppermute x32 -> x0, waiting for transfers between devices: 83.2 us -> none  [shifted(): return lax.ppermute(block, axis, route)]
    dynamic_update_slice x4 -> x0, local copies, waits for them, and re-layouts: 24.2 us -> none  [visit(): lax.dynamic_update_slice(grad_band, previous + jnp.stack([term_real, term...]
    reduce_scatter x2 -> x0, waiting for transfers between devices: 22.5 us -> none  [on_device(): lax.psum_scatter(disperse(grad_band, reach, tile_rows), 'tile', scatter_d...]
    all_gather x2 -> x0, blocking collectives: 22.3 us -> none  [on_device(): band = assemble(lax.all_gather(field, 'tile', axis=2, tiled=True), reach)]
  transfers between devices with their start and end apart: 36 -> 0, of which waited for: 17 -> 0; matrix products, arithmetic and copies ran while one was open for 2% -> 0% of each run, Pallas kernels for 0% -> 0%
where the time goes in v2:
time: 143 us; the launch traced here: 142 us
  Pallas kernels  135 us (94%)
  local copies, waits for them, and re-layouts  4.81 us (3%)
  other arithmetic  2.21 us (2%)
    pallas_call x1, Pallas kernels, on_device(): pl.pallas_call(functools.partial(iterations_kernel, names, reach, chips_z...  135 us
    unnamed x2, local copies, waits for them, and re-layouts  4.21 us

profile of v2, /device:TPU:1, one launch (start us, length us, event | category | flops | bytes accessed | tf_op | source)
XLA Modules:
  0.0 142.3 jit_solution(2397207060704829616)
XLA Ops:
  0.6 0.7 iota_compare_fusion
  1.4 0.8 select_reduce_fusion
  2.2 0.7 slice_reduce_fusion
  2.8 0.6 scatter.4.refs_1_
  3.4 134.6 %shard_map.77 = (f32[2,32,256]{2,1,0:T(8,128)}, f32[1536,256]{1,0:T(8,128)}) custom-call(s32[2]{0:T(128)} %get-tuple-element.19.refs_0_, s32[8,128]{1,0:T(8,128)} %scatter.4.refs_1_, f32[2,32,256]{2,1,0:T(8,128)} %refs_2_.1, f32[1536,256]{1,0:T(8,128)} %bitcast.3, f32[2,256,256]{2,1,0:T(8,128)} %refs_4_.1, bf16[9,256,256]{2,1,0:T(8,128)(2,1)} %constant.40.clone.refs_5_), custom_call_target="tpu_custom_call" | custom-call | tf_op jit(solution)/shard_map/pallas_call | solution.py:674
  138.1 1.5 %copy.11 = f32[2,32,256]{2,1,0:T(8,128)} copy(f32[2,32,256]{2,1,0:T(8,128)} %get-tuple-element.22) | data formatting | bytes 131072
  139.6 2.7 %copy.12 = f32[2,3,256,256]{3,2,1,0:T(8,128)} copy(f32[2,3,256,256]{3,2,1,0:T(8,128)} %bitcast.4) | data formatting | bytes 3145728

commit v3 on v2

--- a/solution.py
+++ b/solution.py
@@ -19,6 +19,7 @@
 CHIPS_Z = 8
 LANES = 128
 MESH = pl.DeviceIdType.MESH
+STAGED = ("positions", "field", "modes", "amplitude", "tables")
 VMEM_LIMIT = 56 * 1024 * 1024
 
 
@@ -107,6 +108,10 @@
         return jnp.logical_and(other >= 0, other < self.scans), (other, self.tile)
 
 
+def around(size):
+    return sorted(range(1, size), key=lambda k: -min(k, size - k))
+
+
 def distances(reach):
     far_first = sorted(range(1, reach + 1), reverse=True)
     return [sign * d for d in far_first for sign in (1, -1)]
@@ -126,7 +131,7 @@
                 pl.semaphore_signal(barrier, inc=1, device_id=device, device_id_type=MESH)
 
             total = total + condition.astype(jnp.int32)
-    pl.semaphore_wait(barrier, total)
+    return lambda: pl.semaphore_wait(barrier, total)
 
 
 def sublane(shape):
@@ -247,9 +252,10 @@
 
 def iterations_kernel(names, reach, chips_z, owners, rate, *refs):
     at_name = dict(zip(names, refs))
-    first_field, first_modes = at_name["field"], at_name["modes"]
-    rows_ref, amplitude, tables = at_name["rows"], at_name["amplitude"], at_name["tables"]
-    columns, table = at_name["columns"], at_name["table"]
+    held = {name: at_name["held_" + name] for name in STAGED}
+    first_field, first_modes = held["field"], held["modes"]
+    amplitude, tables = held["amplitude"], held["tables"]
+    notes_of, table = at_name["notes_of"], at_name["table"]
     place = Place(chips_z)
     _, rows, width = first_field.shape
     slots, patch = amplitude.shape[0], amplitude.shape[1]
@@ -295,13 +301,17 @@
         )
         partners.append((meets, device))
     partners += [place.near(d) for d in order]
-    greet(partners)
+    everyone_here = greet(partners)
+    staged = {}
+    for at, name in enumerate(STAGED):
+        staged[name] = pltpu.make_async_copy(at_name[name], held[name], at_name["staged"].at[at])
+        staged[name].start()
 
     def share_strip(it, field):
         strip = at_name["strip"].at[it]
         own = pl.ds(pl.multiple_of(place.tile * width, LANES), width)
         copies = []
-        for k in range(1, ys):
+        for k in around(ys):
             copy = copy_to(field, strip.at[:, :, own], place.ring_tile(k)[1], "strip", it, k - 1)
             send(copy)
             copies.append(copy)
@@ -310,7 +320,7 @@
 
     def cut(it, source, slot, target):
         strip = at_name["strip"].at[it]
-        column = columns[source, 0, slot]
+        column = notes_of[source, 1, slot]
         first = column // LANES
         inside = column - first * LANES
         for p in range(2):
@@ -362,7 +372,7 @@
         arrived = at_name["arrived"].at[it, slot]
 
         def place_window(source, carry):
-            column = columns[source, 0, slot]
+            column = notes_of[source, 1, slot]
             first = column // LANES
             inside = column - first * LANES
             for p in range(2):
@@ -385,14 +395,6 @@
         for exists, copy in copies:
             pl.when(exists)(copy.wait_recv)
 
-    strip_copies = share_strip(0, first_field)
-    table[reach] = at_name["own_columns"][...]
-    notes = []
-    for at, d in enumerate(order):
-        exists, device = place.near(d)
-        copy = copy_to(at_name["own_columns"], table.at[reach - d], device, "note", at)
-        send(copy, exists)
-        notes.append((place.near(-d)[0], copy))
     for d in order:
 
         @pl.when(jnp.logical_not(place.near(-d)[0]))
@@ -406,13 +408,36 @@
                     at_name["arrived"][it, slot, reach - d] = jnp.zeros((2, rows, patch), jnp.float32)
 
     at_name["grad_strip"][...] = jnp.zeros(at_name["grad_strip"].shape, jnp.float32)
+    staged["positions"].wait()
+    position = held["positions"][...].astype(jnp.float32)
+    index = lax.broadcasted_iota(jnp.int32, position.shape, 1)
+    note_at = [lax.broadcasted_iota(jnp.int32, table.shape[1:], axis) for axis in range(2)]
+    note = jnp.zeros(table.shape[1:], jnp.float32)
+    for slot in range(slots):
+        found = jnp.sum(jnp.where(index == at_name["scan_list"][slot], position, 0.0), axis=1, keepdims=True)
+        for p in range(2):
+            here = jnp.logical_and(note_at[0] == p, note_at[1] == slot)
+            note = jnp.where(here, jnp.broadcast_to(found[p : p + 1], note.shape), note)
+    table[reach] = note.astype(jnp.int32)
+    staged["field"].wait()
+    everyone_here()
+
+    strip_copies = share_strip(0, first_field)
+    notes = []
+    for at, d in enumerate(order):
+        exists, device = place.near(d)
+        copy = copy_to(table.at[reach], table.at[reach - d], device, "note", at)
+        send(copy, exists)
+        notes.append((place.near(-d)[0], copy))
     wait_near(notes)
-    local = pltpu.make_async_copy(table, columns, at_name["local"])
+    local = pltpu.make_async_copy(table, notes_of, at_name["local"])
     local.start()
     local.wait()
     for copy in strip_copies:
         copy.wait_recv()
     window_copies = [send_windows(0, slot) for slot in range(slots)]
+    for name in ("modes", "amplitude", "tables"):
+        staged[name].wait()
 
     for it in range(ITERATIONS):
         last = it == ITERATIONS - 1
@@ -426,7 +451,7 @@
         for slot in range(slots):
             wait_near(window_copies[slot])
             slot_gradient(
-                rows_ref[slot], at_name["window"].at[it, slot], modes, amplitude.at[slot], tables,
+                notes_of[reach, 0, slot] - place.scan * rows + patch // 2, at_name["window"].at[it, slot], modes, amplitude.at[slot], tables,
                 at_name["grad"].at[it, slot], grad_modes, at_name["patch"], at_name["pattern"], slot,
             )
             if slot < slots - 1:
@@ -435,7 +460,7 @@
         mine, other = place.core * half, (1 - place.core) * half
         core_part, core_sum = at_name["core_part"].at[it], at_name["core_sum"].at[it]
         core_copies = []
-        for k in range(1, max(xs, ys) + 1):
+        for k in around(max(xs, ys)) + [max(xs, ys)]:
             for c, (axis, _) in enumerate(chains):
                 here, size = place.along(axis)
                 if k > size:
@@ -461,9 +486,10 @@
                 )
                 send(copy)
                 one_copies[c].append(copy)
-        for slot in range(slots - 1):
-            wait_near(grad_copies[slot])
-            place_windows(it, slot)
+        if not last:
+            for slot in range(slots - 1):
+                wait_near(grad_copies[slot])
+                place_windows(it, slot)
         two_copies = [[], []]
         for c, (axis, axis_two) in enumerate(chains):
             here, size = place.along(axis)
@@ -475,7 +501,7 @@
                 total = total + at_name["one_parts"][it, c, k, :quarter, :]
             one_sum = at_name["one_sum"].at[it, c, pl.ds(0, quarter)]
             one_sum[...] = total
-            for k in range(1, place.along(axis_two)[1]):
+            for k in around(place.along(axis_two)[1]):
                 to, device = place.ring(axis_two, k)
                 copy = copy_to(
                     one_sum.at[rows_at(to * part, part)], at_name["two_parts"].at[it, c, k - 1],
@@ -484,19 +510,32 @@
                 send(copy)
                 two_copies[c].append(copy)
 
-        wait_near(grad_copies[slots - 1])
-        place_windows(it, slots - 1)
         grad_strip = at_name["grad_strip"].at[it]
         tile_copies = []
-        for k in range(1, ys):
-            y, device = place.ring_tile(k)
-            copy = copy_to(
-                grad_strip.at[:, :, pl.ds(pl.multiple_of(y * width, LANES), width)],
-                at_name["tile_parts"].at[it, k - 1], device, "tile", it, k - 1,
-            )
-            send(copy)
-            tile_copies.append(copy)
-
+
+        def sum_windows(slot_range):
+            for slot in slot_range:
+                wait_near(grad_copies[slot])
+                place_windows(it, slot)
+            for k in around(ys):
+                y, device = place.ring_tile(k)
+                copy = copy_to(
+                    grad_strip.at[:, :, pl.ds(pl.multiple_of(y * width, LANES), width)],
+                    at_name["tile_parts"].at[it, k - 1], device, "tile", it, k - 1,
+                )
+                send(copy)
+                tile_copies.append(copy)
+
+        def update_field():
+            for copy in tile_copies:
+                copy.wait_recv()
+            total = grad_strip[:, :, pl.ds(pl.multiple_of(place.tile * width, LANES), width)]
+            for k in range(ys - 1):
+                total = total + at_name["tile_parts"][it, k]
+            new_field[...] = field[...] - OBJECT_RATE * total
+
+        if not last:
+            sum_windows(range(slots - 1, slots))
         z_copies = [[], []]
         for c, (_, axis_two) in enumerate(chains):
             here, size = place.along(axis_two)
@@ -507,7 +546,7 @@
                 total = total + at_name["two_parts"][it, c, k]
             two_sum = at_name["two_sum"].at[it, c]
             two_sum[...] = total
-            for k in range(1, zs):
+            for k in around(zs):
                 z, device = place.ring_z(k)
                 owned = owns(c, z)
                 copy = copy_to(
@@ -517,13 +556,10 @@
                 send(copy, owned < owners)
                 z_copies[c].append(copy)
 
-        for copy in tile_copies:
-            copy.wait_recv()
-        total = grad_strip[:, :, pl.ds(pl.multiple_of(place.tile * width, LANES), width)]
-        for k in range(ys - 1):
-            total = total + at_name["tile_parts"][it, k]
-        new_field[...] = field[...] - OBJECT_RATE * total
-        if not last:
+        if last:
+            sum_windows(range(slots))
+        else:
+            update_field()
             strip_copies = share_strip(it + 1, new_field)
 
         my_quarters, my_parts, zg_copies = [], [], [[], []]
@@ -547,7 +583,7 @@
                 at = rows_at(my_part + my_piece, piece)
                 new_modes[at, :] = modes[at, :] - rate * total
 
-            for k in range(1, zs):
+            for k in around(zs):
                 ref = new_modes.at[rows_at(my_part + my_piece, piece)]
                 copy = copy_to(ref, ref, place.ring_z(k)[1], "zg", it, c, k - 1)
                 send(copy, owner)
@@ -555,35 +591,39 @@
         two_copies = [[], []]
         for c, (_, axis_two) in enumerate(chains):
             wait_near(zg_copies[c])
-            for k in range(1, place.along(axis_two)[1]):
+            for k in around(place.along(axis_two)[1]):
                 ref = new_modes.at[rows_at(my_parts[c], part)]
                 copy = copy_to(ref, ref, place.ring(axis_two, k)[1], "twog", it, c, k - 1)
                 send(copy)
                 two_copies[c].append(copy)
-        if not last:
+        if last:
+            update_field()
+        else:
             for copy in strip_copies:
                 copy.wait_recv()
-            window_copies = [send_windows(it + 1, slot) for slot in range(slots)]
-        one_copies, core_copies = [[], []], []
+            window_copies = [send_windows(it + 1, 0)]
+        one_copies, core_copies = [{}, {}], []
         for c, (axis, _) in enumerate(chains):
             for copy in two_copies[c]:
                 copy.wait_recv()
             here, size = place.along(axis)
             quarter = chain // size
             ref = new_modes.at[rows_at(my_quarters[c], quarter)]
-            for k in range(1, size):
+            for k in around(size):
                 copy = copy_to(ref, ref, place.ring(axis, k)[1], "oneg", it, c, k - 1)
                 send(copy)
-                one_copies[c].append(copy)
+                one_copies[c][k] = copy
             copy = copy_to(ref, ref, place.at_core(), "coreg", it, c, 0)
             send(copy)
             core_copies.append(copy)
-        for k in range(1, max(xs, ys)):
+        if not last:
+            window_copies += [send_windows(it + 1, slot) for slot in range(1, slots)]
+        for k in around(max(xs, ys))[::-1]:
             for c, (axis, _) in enumerate(chains):
                 here, size = place.along(axis)
                 if k >= size:
                     continue
-                one_copies[c][k - 1].wait_recv()
+                one_copies[c][k].wait_recv()
                 quarter = chain // size
                 start = mine + c * chain + lax.rem(here + size - k, size) * quarter
                 ref = new_modes.at[rows_at(start, quarter)]
@@ -594,6 +634,31 @@
             copy.wait_recv()
     for wait in finish:
         wait()
+
+
+def hand_over_kernel(field_ref, modes_ref, field_out, modes_out, sems):
+    copies = [
+        pltpu.make_async_copy(field_ref, field_out, sems.at[0]),
+        pltpu.make_async_copy(modes_ref, modes_out, sems.at[1]),
+    ]
+    for copy in copies:
+        copy.start()
+    for copy in copies:
+        copy.wait()
+
+
+def handed_over(field, modes):
+    vmem, anywhere = pl.BlockSpec(memory_space=pltpu.VMEM), pl.BlockSpec(memory_space=pl.ANY)
+    return pl.pallas_call(
+        hand_over_kernel,
+        out_shape=(
+            jax.ShapeDtypeStruct(field.shape, jnp.float32),
+            jax.ShapeDtypeStruct(modes.shape, jnp.float32),
+        ),
+        in_specs=[vmem, vmem],
+        out_specs=(anywhere, anywhere),
+        scratch_shapes=[pltpu.SemaphoreType.DMA((2,))],
+    )(field, modes)
 
 
 def on_device(chips_z, object_field, probe, amplitude, positions, scan_list):
@@ -615,10 +680,6 @@
     quarter = chain // min(chips_x, tiles)
 
     tables = jnp.asarray(dft_tables(patch))
-    match = scan_list[:, None] == jnp.arange(total, dtype=jnp.int32)[None, :]
-    found = jnp.sum(jnp.where(match[:, :, None], positions[None], 0), axis=1)
-    row_start = found[:, 0] - lax.axis_index("scan") * rows + patch // 2
-    own_columns = jnp.zeros((8, LANES), jnp.int32).at[0, :slots].set(found[:, 1])
 
     def vmem(*shape):
         return pltpu.VMEM((ITERATIONS,) + shape, jnp.float32)
@@ -626,7 +687,7 @@
     band = (2, (near + 1) * rows, patch)
     block = (2, rows, patch)
     scratch = {
-        "columns": pltpu.SMEM((near + 1, 8, LANES), jnp.int32),
+        "notes_of": pltpu.SMEM((near + 1, 8, LANES), jnp.int32),
         "table": pltpu.VMEM((near + 1, 8, LANES), jnp.int32),
         "strip": vmem(2, rows, width * tiles),
         "outgoing": vmem(slots, near, *block),
@@ -648,6 +709,7 @@
         "two_sum": vmem(2, part, patch),
         "z_parts": vmem(2, chips_z - 1, piece, patch),
         "local": pltpu.SemaphoreType.DMA(()),
+        "staged": pltpu.SemaphoreType.DMA((len(STAGED),)),
     }
     counts = {
         "note": (near,),
@@ -667,7 +729,16 @@
     for name, shape in counts.items():
         scratch[name + "_send"] = pltpu.SemaphoreType.DMA(shape)
         scratch[name + "_recv"] = pltpu.SemaphoreType.DMA(shape)
-    inputs = ["rows", "own_columns", "field", "modes", "amplitude", "tables"]
+    operands = {
+        "positions": positions.T,
+        "field": object_field,
+        "modes": probe.reshape(flat),
+        "amplitude": amplitude,
+        "tables": tables,
+    }
+    for name in STAGED:
+        scratch["held_" + name] = pltpu.VMEM(operands[name].shape, operands[name].dtype)
+    inputs = ["scan_list"] + list(STAGED)
     outputs = ["new_field", "new_modes"]
     names = inputs + outputs + list(scratch)
     in_vmem = pl.BlockSpec(memory_space=pltpu.VMEM)
@@ -677,13 +748,15 @@
             jax.ShapeDtypeStruct(object_field.shape, jnp.float32),
             jax.ShapeDtypeStruct(flat, jnp.float32),
         ),
-        in_specs=[pl.BlockSpec(memory_space=pltpu.SMEM)] + [in_vmem] * 5,
+        in_specs=[pl.BlockSpec(memory_space=pltpu.SMEM)]
+        + [pl.BlockSpec(memory_space=pl.ANY)] * len(STAGED),
         out_specs=(in_vmem, in_vmem),
         scratch_shapes=list(scratch.values()),
         compiler_params=pltpu.CompilerParams(
             collective_id=1, has_side_effects=True, vmem_limit_bytes=VMEM_LIMIT
         ),
-    )(row_start, own_columns, object_field, probe.reshape(flat), amplitude, tables)
+    )(scan_list, *[operands[name] for name in STAGED])
+    field, modes = handed_over(field, modes)
     return field, modes.reshape(probe.shape)
 
 

time: 143 us -> 132 us (0.923)
  local copies, waits for them, and re-layouts: 4.81 us -> 0 us
  Pallas kernels: 135 us -> 131 us
  other arithmetic: 2.21 us -> 0 us
    pallas_call x1, Pallas kernels: 135 us -> 129 us  [on_device(): pl.pallas_call(functools.partial(iterations_kernel, names, reach, chips_z...]
    unnamed x2 -> x0, local copies, waits for them, and re-layouts: 4.21 us -> none
    pallas_call x0 -> x1, Pallas kernels: none -> 2.63 us  [handed_over(): pl.pallas_call(hand_over_kernel, out_shape=(jax.ShapeDtypeStruct(field.sh...]
where the time goes in v3:
time: 132 us
  Pallas kernels  131 us (99%)
    pallas_call x1, Pallas kernels, on_device(): pl.pallas_call(functools.partial(iterations_kernel, names, reach, chips_z...  129 us

profile of v3, /device:TPU:1, one launch (start us, length us, event | category | flops | bytes accessed | tf_op | source)
XLA Modules:
  0.0 132.1 jit_solution(7776464162485737107)
XLA Ops:
  0.6 128.7 %shard_map.77 = (f32[2,32,256]{2,1,0:T(8,128)}, f32[1536,256]{1,0:T(8,128)}) custom-call(s32[2]{0:T(128)} %refs_0_.1, s32[2,512]{1,0:T(2,128)} %bitcast.4, f32[2,32,256]{2,1,0:T(8,128)} %refs_2_.1, f32[1536,256]{1,0:T(8,128)} %bitcast.3, f32[2,256,256]{2,1,0:T(8,128)} %refs_4_.1, bf16[9,256,256]{2,1,0:T(8,128)(2,1)} %constant.2.clone.refs_5_), custom_call_target="tpu_custom_call" | custom-call | tf_op jit(solution)/shard_map/pallas_call | solution.py:745
  129.3 2.6 %shard_map.78 = (f32[2,32,256]{2,1,0:T(8,128)}, f32[1536,256]{1,0:T(8,128)}) custom-call(f32[2,32,256]{2,1,0:T(8,128)} %get-tuple-element.6.field_ref, f32[1536,256]{1,0:T(8,128)} %get-tuple-element.7.modes_ref), custom_call_target="tpu_custom_call" | custom-call | tf_op jit(solution)/shard_map/pallas_call | solution.py:652

commit v4 on v3

--- a/solution.py
+++ b/solution.py
@@ -168,7 +168,7 @@
     return band.reshape((groups + margin) * 8, width)
 
 
-def slot_gradient(row, window, modes, amplitude, tables, grad, grad_modes, patch_ref, pattern_ref, slot):
+def slot_gradient(row, window, modes, patterns, tables, grad, grad_modes, patch_ref, slot):
     patch = patch_ref.shape[1]
     count = modes.shape[0] // (2 * patch)
     half = patch // 2
@@ -204,13 +204,9 @@
             far[p].append(value)
             square = value[:half] * value[:half] + value[half:] * value[half:]
             power[p] = square if power[p] is None else power[p] + square
-    pattern = permuted(amplitude[...], tables[8])
-    pattern_ref[0] = pattern[:, :half]
-    pattern_ref[1] = pattern[:, half:]
     factor = []
     for p in range(2):
-        pattern = beside([pattern_ref[q, pl.ds(p, half, stride=2), :] for q in range(2)])
-        value = 1.0 - pattern * lax.rsqrt(jnp.maximum(power[p], INTENSITY_FLOOR))
+        value = 1.0 - patterns[p] * lax.rsqrt(jnp.maximum(power[p], INTENSITY_FLOOR))
         factor.append(stacked([value, value]))
     pieces = [[], []]
     for m in range(count):
@@ -438,6 +434,14 @@
     window_copies = [send_windows(0, slot) for slot in range(slots)]
     for name in ("modes", "amplitude", "tables"):
         staged[name].wait()
+    for slot in range(slots):
+        pattern = permuted(amplitude[slot], tables[8])
+        for q in range(2):
+            at_name["pattern"][slot, q] = pattern[:, q * (patch // 2) : (q + 1) * (patch // 2)]
+        for p in range(2):
+            at_name["patterns"][slot, p] = beside(
+                [at_name["pattern"][slot, q, pl.ds(p, patch // 2, stride=2), :] for q in range(2)]
+            )
 
     for it in range(ITERATIONS):
         last = it == ITERATIONS - 1
@@ -451,8 +455,8 @@
         for slot in range(slots):
             wait_near(window_copies[slot])
             slot_gradient(
-                notes_of[reach, 0, slot] - place.scan * rows + patch // 2, at_name["window"].at[it, slot], modes, amplitude.at[slot], tables,
-                at_name["grad"].at[it, slot], grad_modes, at_name["patch"], at_name["pattern"], slot,
+                notes_of[reach, 0, slot] - place.scan * rows + patch // 2, at_name["window"].at[it, slot], modes, at_name["patterns"].at[slot], tables,
+                at_name["grad"].at[it, slot], grad_modes, at_name["patch"], slot,
             )
             if slot < slots - 1:
                 grad_copies.append(send_gradient(it, slot))
@@ -589,30 +593,38 @@
                 send(copy, owner)
                 zg_copies[c].append((owns(c, lax.rem(place.z + zs - k, zs)) < owners, copy))
         two_copies = [[], []]
+        one_copies, core_copies = [{}, {}], []
+
+        def pass_on(c, which, start):
+            axis = chains[c][0]
+            ref = new_modes.at[rows_at(start, part)]
+            for k in around(place.along(axis)[1]):
+                copy = copy_to(ref, ref, place.ring(axis, k)[1], "oneg", it, c, k - 1, which)
+                send(copy)
+                one_copies[c][k, which] = copy
+
         for c, (_, axis_two) in enumerate(chains):
             wait_near(zg_copies[c])
             for k in around(place.along(axis_two)[1]):
                 ref = new_modes.at[rows_at(my_parts[c], part)]
                 copy = copy_to(ref, ref, place.ring(axis_two, k)[1], "twog", it, c, k - 1)
                 send(copy)
-                two_copies[c].append(copy)
+                two_copies[c].append((k, copy))
+            pass_on(c, 0, my_parts[c])
         if last:
             update_field()
         else:
             for copy in strip_copies:
                 copy.wait_recv()
             window_copies = [send_windows(it + 1, 0)]
-        one_copies, core_copies = [{}, {}], []
-        for c, (axis, _) in enumerate(chains):
-            for copy in two_copies[c]:
+        for c, (axis, axis_two) in enumerate(chains):
+            here_two, size_two = place.along(axis_two)
+            for k, copy in reversed(two_copies[c]):
                 copy.wait_recv()
+                pass_on(c, k, my_quarters[c] + lax.rem(here_two + size_two - k, size_two) * part)
             here, size = place.along(axis)
             quarter = chain // size
             ref = new_modes.at[rows_at(my_quarters[c], quarter)]
-            for k in around(size):
-                copy = copy_to(ref, ref, place.ring(axis, k)[1], "oneg", it, c, k - 1)
-                send(copy)
-                one_copies[c][k] = copy
             copy = copy_to(ref, ref, place.at_core(), "coreg", it, c, 0)
             send(copy)
             core_copies.append(copy)
@@ -623,7 +635,8 @@
                 here, size = place.along(axis)
                 if k >= size:
                     continue
-                one_copies[c][k].wait_recv()
+                for which in range(place.along(chains[c][1])[1]):
+                    one_copies[c][k, which].wait_recv()
                 quarter = chain // size
                 start = mine + c * chain + lax.rem(here + size - k, size) * quarter
                 ref = new_modes.at[rows_at(start, quarter)]
@@ -699,7 +712,8 @@
         "field_between": pltpu.VMEM(object_field.shape, jnp.float32),
         "modes_between": pltpu.VMEM(flat, jnp.float32),
         "patch": pltpu.VMEM((2, patch, patch), jnp.float32),
-        "pattern": pltpu.VMEM((2, patch, patch // 2), jnp.float32),
+        "pattern": pltpu.VMEM((slots, 2, patch, patch // 2), jnp.float32),
+        "patterns": pltpu.VMEM((slots, 2, patch // 2, patch), jnp.float32),
         "grad_modes": vmem(*flat),
         "core_part": vmem(half, patch),
         "core_sum": vmem(half, patch),
@@ -723,7 +737,7 @@
         "z": (ITERATIONS, 2, chips_z - 1),
         "zg": (ITERATIONS, 2, chips_z - 1),
         "twog": (ITERATIONS, 2, longest - 1),
-        "oneg": (ITERATIONS, 2, longest - 1),
+        "oneg": (ITERATIONS, 2, longest - 1, longest),
         "coreg": (ITERATIONS, 2, longest),
     }
     for name, shape in counts.items():

time: 132 us -> 130 us (0.985)
  Pallas kernels: 131 us -> 129 us
    pallas_call x1, Pallas kernels: 129 us -> 126 us  [on_device(): pl.pallas_call(functools.partial(iterations_kernel, names, reach, chips_z...]
where the time goes in v4:
time: 130 us; the launch traced here: 129 us
  Pallas kernels  129 us (99%)
    pallas_call x1, Pallas kernels, on_device(): pl.pallas_call(functools.partial(iterations_kernel, names, reach, chips_z...  126 us
    pallas_call x1, Pallas kernels, handed_over(): pl.pallas_call(hand_over_kernel, out_shape=(jax.ShapeDtypeStruct(field.sh...  2.63 us

profile of v4, /device:TPU:1, one launch (start us, length us, event | category | flops | bytes accessed | tf_op | source)
XLA Modules:
  0.0 129.5 jit_solution(10665905158723639364)
XLA Ops:
  0.6 126.0 %shard_map.77 = (f32[2,32,256]{2,1,0:T(8,128)}, f32[1536,256]{1,0:T(8,128)}) custom-call(s32[2]{0:T(128)} %refs_0_.1, s32[2,512]{1,0:T(2,128)} %bitcast.4, f32[2,32,256]{2,1,0:T(8,128)} %refs_2_.1, f32[1536,256]{1,0:T(8,128)} %bitcast.3, f32[2,256,256]{2,1,0:T(8,128)} %refs_4_.1, bf16[9,256,256]{2,1,0:T(8,128)(2,1)} %constant.2.clone.refs_5_), custom_call_target="tpu_custom_call" | custom-call | tf_op jit(solution)/shard_map/pallas_call | solution.py:759
  126.7 2.6 %shard_map.78 = (f32[2,32,256]{2,1,0:T(8,128)}, f32[1536,256]{1,0:T(8,128)}) custom-call(f32[2,32,256]{2,1,0:T(8,128)} %get-tuple-element.6.field_ref, f32[1536,256]{1,0:T(8,128)} %get-tuple-element.7.modes_ref), custom_call_target="tpu_custom_call" | custom-call | tf_op jit(solution)/shard_map/pallas_call | solution.py:665

commit v5 on v4

--- a/solution.py
+++ b/solution.py
@@ -484,12 +484,16 @@
             at = rows_at(start, quarter)
             core_sum[at, :] = core_part[at, :] + grad_modes[rows_at(mine + start, quarter), :]
             if k < size:
-                copy = copy_to(
-                    core_sum.at[at], at_name["one_parts"].at[it, c, k - 1, pl.ds(0, quarter)],
-                    place.ring(axis, k)[1], "one", it, c, k - 1,
-                )
-                send(copy)
-                one_copies[c].append(copy)
+                here_two, size_two = place.along(chains[c][1])
+                for which in around(size_two) + [0]:
+                    offset = lax.rem(here_two + which, size_two) * part
+                    copy = copy_to(
+                        core_sum.at[rows_at(start + offset, part)],
+                        at_name["one_parts"].at[it, c, k - 1, rows_at(offset, part)],
+                        place.ring(axis, k)[1], "one", it, c, k - 1, which,
+                    )
+                    send(copy)
+                    one_copies[c].append((which, copy))
         if not last:
             for slot in range(slots - 1):
                 wait_near(grad_copies[slot])
@@ -498,15 +502,19 @@
         for c, (axis, axis_two) in enumerate(chains):
             here, size = place.along(axis)
             quarter = chain // size
-            for copy in one_copies[c]:
-                copy.wait_recv()
-            total = core_sum[rows_at(c * chain + here * quarter, quarter), :]
-            for k in range(size - 1):
-                total = total + at_name["one_parts"][it, c, k, :quarter, :]
             one_sum = at_name["one_sum"].at[it, c, pl.ds(0, quarter)]
-            one_sum[...] = total
-            for k in around(place.along(axis_two)[1]):
+            for k in around(place.along(axis_two)[1]) + [0]:
+                for which, copy in one_copies[c]:
+                    if which == k:
+                        copy.wait_recv()
                 to, device = place.ring(axis_two, k)
+                at = rows_at(to * part, part)
+                total = core_sum[rows_at(c * chain + here * quarter + to * part, part), :]
+                for i in range(size - 1):
+                    total = total + at_name["one_parts"][it, c, i, at, :]
+                one_sum[at, :] = total
+                if k == 0:
+                    continue
                 copy = copy_to(
                     one_sum.at[rows_at(to * part, part)], at_name["two_parts"].at[it, c, k - 1],
                     device, "two", it, c, k - 1,
@@ -732,7 +740,7 @@
         "grad": (ITERATIONS, slots, near),
         "tile": (ITERATIONS, tiles - 1),
         "core": (ITERATIONS, 2, longest),
-        "one": (ITERATIONS, 2, longest - 1),
+        "one": (ITERATIONS, 2, longest - 1, longest),
         "two": (ITERATIONS, 2, longest - 1),
         "z": (ITERATIONS, 2, chips_z - 1),
         "zg": (ITERATIONS, 2, chips_z - 1),

time: 130 us -> 130 us (level)
  no operation moved by 1% of the time
where the time goes in v5:
time: 130 us; the launch traced here: 129 us
  Pallas kernels  129 us (99%)
    pallas_call x1, Pallas kernels, on_device(): pl.pallas_call(functools.partial(iterations_kernel, names, reach, chips_z...  126 us
    pallas_call x1, Pallas kernels, handed_over(): pl.pallas_call(hand_over_kernel, out_shape=(jax.ShapeDtypeStruct(field.sh...  2.63 us

profile of v5, /device:TPU:1, one launch (start us, length us, event | category | flops | bytes accessed | tf_op | source)
XLA Modules:
  0.0 129.4 jit_solution(3550868103670295493)
XLA Ops:
  0.6 126.0 %shard_map.77 = (f32[2,32,256]{2,1,0:T(8,128)}, f32[1536,256]{1,0:T(8,128)}) custom-call(s32[2]{0:T(128)} %refs_0_.1, s32[2,512]{1,0:T(2,128)} %bitcast.4, f32[2,32,256]{2,1,0:T(8,128)} %refs_2_.1, f32[1536,256]{1,0:T(8,128)} %bitcast.3, f32[2,256,256]{2,1,0:T(8,128)} %refs_4_.1, bf16[9,256,256]{2,1,0:T(8,128)(2,1)} %constant.2.clone.refs_5_), custom_call_target="tpu_custom_call" | custom-call | tf_op jit(solution)/shard_map/pallas_call | solution.py:767
  126.6 2.6 %shard_map.78 = (f32[2,32,256]{2,1,0:T(8,128)}, f32[1536,256]{1,0:T(8,128)}) custom-call(f32[2,32,256]{2,1,0:T(8,128)} %get-tuple-element.6.field_ref, f32[1536,256]{1,0:T(8,128)} %get-tuple-element.7.modes_ref), custom_call_target="tpu_custom_call" | custom-call | tf_op jit(solution)/shard_map/pallas_call | solution.py:673
